TPU v7x, 32 devices: a whole 2x2x4 slice. The times are simulated.
32 devices in a mesh: gx: 2 (over core), gy: 4 (over y, x), vec: 4 (over z).
Axes of the slice: x: 2, y: 2, z: 4, core: 2. Of those that a mesh axis runs over, the one named last changes fastest.
Arguments:
- field: float32 [2, 64, 512], P(None, 'gx', 'gy'), may hold values from -4 to 4
- tangents: float32 [1024, 2, 64, 512], P('vec', None, 'gx', 'gy'), as said below
Outputs:
- field_next: float32 [2, 64, 512], P(None, 'gx', 'gy')
- vectors_next: float32 [1024, 2, 64, 512], P('vec', None, 'gx', 'gy')
Inputs may be any that keep to these rules, and one draw needn't show every extreme that they name: `tangents`: real values; no vector is a combination of others.
All inputs are finite; a program needn't handle non-finite values.
Results may differ from a plain program's by a relative error of at most 0.0003.
Values sent between devices are 32-bit elements; how exact they have to be, the bound alone decides.
A program may use at most 128 MiB of HBM per device.

v0:
```python
import jax
import jax.numpy as jnp
from jax import lax
from jax.sharding import PartitionSpec as P

time_step = 0.2
coupling = 1.0
kerr_gain = 1.0


def with_halo(cells, sides, width):
    for axis, dim in sides:
        count = lax.axis_size(axis)
        head = lax.slice_in_dim(cells, 0, width, axis=dim)
        tail = lax.slice_in_dim(cells, cells.shape[dim] - width, cells.shape[dim], axis=dim)
        cells = jnp.concatenate(
            [
                lax.ppermute(tail, axis, [(i, (i + 1) % count) for i in range(count)]),
                cells,
                lax.ppermute(head, axis, [((i + 1) % count, i) for i in range(count)]),
            ],
            axis=dim,
        )
    return cells


def broadcast(array, axis, root):
    mine = lax.axis_index(axis) == root
    return lax.psum(jnp.where(mine, array, jnp.zeros_like(array)), axis)


def neighbours(padded):
    return (
        padded[..., :-2, 1:-1]
        + padded[..., 2:, 1:-1]
        + padded[..., 1:-1, :-2]
        + padded[..., 1:-1, 2:]
    )


def field_rate(padded):
    centre = padded[:, 1:-1, 1:-1]
    neighbour_sum = neighbours(padded)
    re_part, im_part = (centre[0], centre[1])
    density = re_part * re_part + im_part * im_part
    return jnp.stack(
        [
            -coupling * neighbour_sum[1] - kerr_gain * density * im_part,
            coupling * neighbour_sum[0] + kerr_gain * density * re_part,
        ]
    )


def tangent_rate(base, padded):
    re_part, im_part = (base[0], base[1])
    neighbour_sum = neighbours(padded)
    centre = padded[:, :, 1:-1, 1:-1]
    re_tan, im_tan = (centre[:, 0], centre[:, 1])
    cross_term = 2.0 * re_part * im_part
    weight_re = 3.0 * re_part * re_part + im_part * im_part
    weight_im = re_part * re_part + 3.0 * im_part * im_part
    rate_re = -coupling * neighbour_sum[:, 1] - kerr_gain * (
        cross_term * re_tan + weight_im * im_tan
    )
    rate_im = coupling * neighbour_sum[:, 0] + kerr_gain * (
        weight_re * re_tan + cross_term * im_tan
    )
    return jnp.stack([rate_re, rate_im], axis=1)


def tendency(padded):
    base = padded[0, :, 1:-1, 1:-1]
    field_part = field_rate(padded[0])
    tangent_part = tangent_rate(base, padded[1:])
    return jnp.concatenate([field_part[None], tangent_part], axis=0)


def inner_sum(left, right):
    return jnp.einsum("vcrs,wcrs->vw", left, right, precision=lax.Precision.HIGHEST)


def apply_rows(matrix, vectors):
    return jnp.einsum("vw,wcrs->vcrs", matrix, vectors, precision=lax.Precision.HIGHEST)


def triangle_inverse(gram_sums, total_dims, size_here):
    factor = jnp.linalg.cholesky(gram_sums / total_dims)
    identity_mat = jnp.eye(size_here, dtype=jnp.float32)
    return jax.scipy.linalg.solve_triangular(factor, identity_mat, lower=True)


def local(field, tangents):
    lattice_rows = field.shape[1]
    lattice_cols = field.shape[2]
    vectors_here = tangents.shape[0]
    total_dims = 2 * lattice_rows * lattice_cols * lax.axis_size("gx") * lax.axis_size("gy")
    stacked = jnp.concatenate([field[None], tangents], axis=0)
    padded_one = with_halo(stacked, (("gx", 2), ("gy", 3)), 1)
    midpoint = stacked + 0.5 * time_step * tendency(padded_one)
    padded_two = with_halo(midpoint, (("gx", 2), ("gy", 3)), 1)
    advanced = stacked + time_step * tendency(padded_two)
    field_next = advanced[0]
    stepped = advanced[1:]
    is_owner = lax.axis_index("vec") == 0
    raw_vectors = broadcast(stepped, "vec", 0)
    gram_sums, cross_sums = lax.psum(
        (inner_sum(raw_vectors, raw_vectors), inner_sum(raw_vectors, stepped)), ("gx", "gy")
    )
    inverse = triangle_inverse(gram_sums, total_dims, vectors_here)
    orthonormal = apply_rows(inverse, raw_vectors)
    coefficients = jnp.dot(inverse, cross_sums / total_dims, precision=lax.Precision.HIGHEST)
    projected = stepped - jnp.einsum(
        "vw,vcrs->wcrs", coefficients, orthonormal, precision=lax.Precision.HIGHEST
    )
    vectors_next = jnp.where(is_owner, orthonormal, projected)
    return (field_next, vectors_next)


def solution(mesh):
    in_specs = (P(None, "gx", "gy"), P("vec", None, "gx", "gy"))
    out_specs = (P(None, "gx", "gy"), P("vec", None, "gx", "gy"))
    return jax.shard_map(local, mesh=mesh, in_specs=in_specs, out_specs=out_specs, check_vma=False)
```

profile of v0, /device:TPU:0, one launch (start us, length us, event | category | flops | bytes accessed | tf_op | source)
XLA Modules:
  0.0 652.4 jit_solution(10527706976731883231)
XLA Ops:
  7.2 8.2 %copy.55 = f32[256,2,32,128]{3,0,2,1:T(8,128)S(1)} copy(f32[256,2,32,128]{3,2,1,0:T(8,128)} %param.3) | data formatting | bytes 16777216 | tf_op args[1]
  16.1 1.1 collective-permute-done
  17.6 1.2 copy-done
  19.7 7.7 %fusion.42 = (f32[257,2,34,1]{3,0,2,1:T(8,128)}, f32[257,2,34,1]{3,0,2,1:T(8,128)}) fusion(f32[257,2,34,128]{3,0,2,1:T(8,128)S(1)} %pad_maximum_fusion.1), kind=kLoop, calls=%fused_computation.130 | loop fusion | bytes 279616 | tf_op jit(solution)/shard_map/slice | solution.py:15
  27.4 6.5 copy.56
  33.9 3.0 collective-permute-start.2
  36.9 6.5 copy.57
  43.4 1.2 collective-permute-start.3
  44.6 5.3 copy.58
  49.9 5.3 copy.59
  55.2 1.5 pad_maximum_fusion.30
  57.5 1.3 slice-done.7
  58.8 19.8 %fusion.5 = f32[256,2,32,128]{3,0,2,1:T(8,128)} fusion(f32[257,2,34,1]{3,0,2,1:T(8,128)} %copy.59, f32[257,2,1,128]{3,0,2,1:T(8,128)S(1)} %collective-permute-done.1, f32[257,2,1,128]{3,0,2,1:T(8,128)S(1)} %collective-permute-done, f32[256,2,32,128]{3,0,2,1:T(8,128)} %copy-done, f32[1,2,32,128]{3,0,2,1:T(1,128)S(1)} %bitcast.85, ...), kind=kLoop, calls=%fused_computation.23 | loop fusion | flops 31457280 | bytes 17476128 | tf_op jit(solution)/shard_map/add | solution.py:34
  78.6 4.4 fusion.11
  83.1 2.9 fusion
  86.0 3.5 copy-done.1
  90.1 1.0 fusion.43
  91.5 3.9 pad_maximum_fusion.2
  95.4 7.7 %fusion.41 = (f32[257,2,34,1]{3,0,2,1:T(8,128)}, f32[257,2,34,1]{3,0,2,1:T(8,128)}) fusion(f32[257,2,34,128]{3,0,2,1:T(8,128)S(1)} %pad_maximum_fusion.2), kind=kLoop, calls=%fused_computation.129 | loop fusion | bytes 279616 | tf_op jit(solution)/shard_map/slice | solution.py:15
  103.1 6.5 copy.71
  109.6 1.1 collective-permute-start.6
  110.7 6.5 copy.72
  117.2 2.3 collective-permute-start.7
  119.6 5.3 copy.73
  124.9 5.3 copy.74
  130.1 1.4 pad_maximum_fusion.26
  132.0 29.8 %fusion.2 = f32[256,2,32,128]{3,0,2,1:T(8,128)} fusion(f32[257,2,34,1]{3,0,2,1:T(8,128)} %copy.74, f32[257,2,1,128]{3,0,2,1:T(8,128)S(1)} %collective-permute-done.5, f32[257,2,32,128]{3,0,2,1:T(8,128)} %copy-done.1, f32[257,2,1,128]{3,0,2,1:T(8,128)S(1)} %collective-permute-done.4, f32[257,2,34,1]{3,0,2,1:T(8,128)} %copy.73), kind=kLoop, calls=%fused_computation.12 | loop fusion | flops 23068672 | bytes 17476128 | tf_op jit(solution)/shard_map/add | solution.py:34
  161.8 7.0 %fusion.10 = (f32[256,1,32,128]{3,0,2,1:T(8,128)S(1)}, f32[256,1,32,128]{3,0,2,1:T(8,128)S(1)}) fusion(f32[256,2,32,128]{3,0,2,1:T(8,128)} %fusion.2, f32[257,2,32,128]{3,0,2,1:T(8,128)} %copy-done.1, f32[32,128]{1,0:T(8,128)S(1)} %get-tuple-element.64, f32[32,128]{1,0:T(8,128)S(1)} %get-tuple-element.66, f32[32,128]{1,0:T(8,128)S(1)} %get-tuple-element.65), kind=kLoop, calls=%fused_computation.45 | loop fusion | flops 9437184 | bytes 25214976 | tf_op jit(solution)/shard_map/sub | solution.py:62
  168.8 4.6 fusion.1
  173.4 3.4 copy-done.3
  176.8 4.7 slice_select_fusion
  181.6 291.7 %all-reduce.5.cloned.1.call-done = f32[256,2,32,128]{3,0,2,1:T(8,128)} async-done(((f32[256,2,32,128]{3,0,2,1:T(8,128)}), f32[256,2,32,128]{3,0,2,1:T(8,128)}) %all-reduce.5.cloned.1.call-update) | async-done | bytes 8388624 | tf_op jit(solution)/shard_map/psum | solution.py:29
  473.3 12.0 %fusion.12 = f32[256,256]{0,1:T(8,128)} fusion(f32[256,2,32,128]{3,0,2,1:T(8,128)} %all-reduce.5.cloned.1.call-done, f32[257,2,32,128]{3,0,2,1:T(8,128)} %copy-done.3), kind=kOutput, calls=%fused_computation.49 | convolution fusion | flops 6442450944 | bytes 17039360 | tf_op jit(solution)/shard_map/vcrs,wcrs->vw/dot_general | solution.py:79
  485.4 7.6 %convolution_bitcast_fusion.1 = f32[256,256]{0,1:T(8,128)} fusion(f32[256,2,32,128]{3,0,2,1:T(8,128)S(1)} %copy-done.2), kind=kOutput, calls=%fused_computation.51 | convolution fusion | flops 6442450944 | bytes 8650752 | tf_op jit(solution)/shard_map/vcrs,wcrs->vw/dot_general | solution.py:79
  493.0 1.6 slice.338
  494.6 52.2 %all-reduce.7.cloned.1.call-done = (f32[256,256]{0,1:T(8,128)}, f32[256,256]{0,1:T(8,128)}) async-done(((f32[256,256]{0,1:T(8,128)}, f32[256,256]{0,1:T(8,128)}), (f32[256,256]{0,1:T(8,128)}, f32[256,256]{0,1:T(8,128)})) %all-reduce.7.cloned.1.call-update) | async-done | bytes 524304 | tf_op jit(solution)/shard_map/psum | solution.py:106
  547.9 1.0 fusion.19
  548.9 11.7 %cholesky.50 = f32[128,128]{1,0:T(8,128)S(1)} custom-call(f32[128,128]{1,0:T(8,128)S(1)} %cholesky.118), custom_call_target="Cholesky" | custom-call | tf_op jit(solution)/shard_map/jit(cholesky)/cholesky | solution.py:87
  560.6 10.0 %custom-call.15 = f32[1,128,128]{1,2,0:T(8,128)S(1)} custom-call(f32[1,128,128]{2,1,0:T(8,128)S(1)} %get-tuple-element.59), custom_call_target="InvertDiagBlocksLowerTriangular" | custom-call | tf_op jit(solution)/shard_map/jit(cholesky)/cholesky | solution.py:87
  571.1 11.7 %cholesky.105 = f32[128,128]{1,0:T(8,128)S(1)} custom-call(f32[128,128]{1,0:T(8,128)S(1)} %convolution_subtract_fusion.1), custom_call_target="Cholesky" | custom-call | tf_op jit(solution)/shard_map/jit(cholesky)/cholesky | solution.py:87
  584.9 3.9 while.1
  585.5 1.4 bitcast_dynamic-update-slice_fusion.2
  587.5 1.4 bitcast_dynamic-update-slice_fusion.2
  588.9 19.7 %custom-call.16 = f32[2,128,128]{1,2,0:T(8,128)S(1)} custom-call(f32[2,128,128]{2,1,0:T(8,128)S(1)} %get-tuple-element.9), custom_call_target="InvertDiagBlocksLowerTriangular" | custom-call | tf_op jit(solution)/shard_map/jit(_solve_triangular)/triangular_solve | solution.py:89
  609.4 1.5 convolution_bitcast_fusion
  611.0 10.8 %fusion.17 = f32[256,2,32,128]{3,0,2,1:T(8,128)S(1)} fusion(f32[256,2,32,128]{3,0,2,1:T(8,128)} %all-reduce.5.cloned.1.call-done, f32[128,256]{1,0:T(8,128)S(1)} %fusion.25, f32[128,256]{1,0:T(8,128)S(1)} %fusion.22), kind=kOutput, calls=%fused_computation.58 | convolution fusion | flops 6442516480 | bytes 17039360 | tf_op jit(solution)/shard_map/vw,wcrs->vcrs/dot_general | solution.py:83
  621.8 11.7 %subtract_select_fusion = f32[256,2,32,128]{3,0,2,1:T(8,128)} fusion(f32[256,2,32,128]{3,0,2,1:T(8,128)S(1)} %fusion.17, f32[257,2,32,128]{3,0,2,1:T(8,128)S(1)} %bitcast.79, pred[]{:T(512)S(6)} %eq.9, f32[256,256,1,1]{0,1,3,2:T(8,128)S(1)} %convolution_bitcast_fusion), kind=kOutput, calls=%fused_computation.37 | convolution fusion | flops 6446645248 | bytes 33816576 | tf_op jit(solution)/shard_map/vw,vcrs->wcrs/dot_general | solution.py:112
  633.5 11.6 %copy.90 = f32[256,2,32,128]{3,2,1,0:T(8,128)} copy(f32[256,2,32,128]{3,0,2,1:T(8,128)} %subtract_select_fusion) | data formatting | bytes 16777216
  (78 shorter events, 8.7 us)
Async XLA Ops:
  7.2 8.3 %copy-start.4 = (f32[2,32,128]{2,1,0:T(8,128)S(1)}, f32[2,32,128]{2,1,0:T(8,128)}, u32[]{:S(2)}) copy-start(f32[2,32,128]{2,1,0:T(8,128)} %param.2) | copy-start | bytes 98308
  7.2 466.1 %all-reduce.5.cloned.1.call-start = ((), (), s32[]{:S(2)}) async-start(), calls=%async_computation | async-start | bytes 16777216 | tf_op jit(solution)/shard_map/psum | solution.py:29
  15.5 3.4 copy-start
  15.5 1.7 collective-permute-start
  16.0 1.6 collective-permute-start.1
  33.9 10.8 %collective-permute-start.2 = (f32[257,2,34,1]{0,1,3,2:T(2,128)S(1)}, f32[257,2,34,1]{0,1,3,2:T(2,128)S(1)}, u32[]{:S(2)}, u32[]{:S(2)}) collective-permute-start(f32[257,2,34,1]{0,1,3,2:T(2,128)S(1)} %copy.56), channel_id=1, source_target_pairs={{0,4},{4,8},{8,12},{12,0},{1,5},{5,9},{9,13},{13,1},{2,6},{6,10},{... | collective-permute-start | bytes 209720 | tf_op jit(solution)/shard_map/ppermute | solution.py:18
  43.4 6.5 %collective-permute-start.3 = (f32[257,2,34,1]{0,1,3,2:T(2,128)S(1)}, f32[257,2,34,1]{0,1,3,2:T(2,128)S(1)}, u32[]{:S(2)}, u32[]{:S(2)}) collective-permute-start(f32[257,2,34,1]{0,1,3,2:T(2,128)S(1)} %copy.57), channel_id=1, source_target_pairs={{4,0},{8,4},{12,8},{0,12},{5,1},{9,5},{13,9},{1,13},{6,2},{10,6},{... | collective-permute-start | bytes 209720 | tf_op jit(solution)/shard_map/ppermute | solution.py:20
  49.9 7.2 %slice-start.5 = ((s8[9191424]{0:T(1024)(128)(4,1)}), s8[802816]{0:T(1024)(128)(4,1)S(1)}, s32[]{:S(2)}) async-start(s8[9191424]{0:T(1024)(128)(4,1)} %bitcast.80), calls=%async_computation.7 | async-start | bytes 1605632
  55.2 2.4 slice-start.6
  55.2 3.6 slice-start.7
  55.2 23.5 %slice-start = ((s8[8388608]{0:T(1024)(128)(4,1)}), s8[4194304]{0:T(1024)(128)(4,1)S(1)}, s32[]{:S(2)}) async-start(s8[8388608]{0:T(1024)(128)(4,1)} %bitcast.76), calls=%async_computation.2 | async-start | bytes 8388608
  58.8 19.8 %slice-start.1 = ((s8[8388608]{0:T(1024)(128)(4,1)}), s8[4194304]{0:T(1024)(128)(4,1)S(1)}, s32[]{:S(2)}) async-start(s8[8388608]{0:T(1024)(128)(4,1)} %bitcast.76), calls=%async_computation.3 | async-start | bytes 8388608
  86.0 3.5 copy-start.1
  89.5 1.6 collective-permute-start.4
  89.6 1.9 collective-permute-start.5
  109.6 10.0 %collective-permute-start.6 = (f32[257,2,34,1]{0,1,3,2:T(2,128)S(1)}, f32[257,2,34,1]{0,1,3,2:T(2,128)S(1)}, u32[]{:S(2)}, u32[]{:S(2)}) collective-permute-start(f32[257,2,34,1]{0,1,3,2:T(2,128)S(1)} %copy.71), channel_id=1, source_target_pairs={{0,4},{4,8},{8,12},{12,0},{1,5},{5,9},{9,13},{13,1},{2,6},{6,10},{... | collective-permute-start | bytes 209720 | tf_op jit(solution)/shard_map/ppermute | solution.py:18
  117.2 7.6 %collective-permute-start.7 = (f32[257,2,34,1]{0,1,3,2:T(2,128)S(1)}, f32[257,2,34,1]{0,1,3,2:T(2,128)S(1)}, u32[]{:S(2)}, u32[]{:S(2)}) collective-permute-start(f32[257,2,34,1]{0,1,3,2:T(2,128)S(1)} %copy.72), channel_id=1, source_target_pairs={{4,0},{8,4},{12,8},{0,12},{5,1},{9,5},{13,9},{1,13},{6,2},{10,6},{... | collective-permute-start | bytes 209720 | tf_op jit(solution)/shard_map/ppermute | solution.py:20
  173.4 3.4 copy-start.3
  181.6 365.2 %all-reduce.7.cloned.1.call-start = ((), (), s32[]{:S(2)}) async-start(), calls=%async_computation.1 | async-start | bytes 1048576 | tf_op jit(solution)/shard_map/psum | solution.py:106
  473.3 12.0 %copy-start.2 = (f32[256,2,32,128]{3,0,2,1:T(8,128)S(1)}, f32[256,2,32,128]{3,0,2,1:T(8,128)}, u32[]{:S(2)}) copy-start(f32[256,2,32,128]{3,0,2,1:T(8,128)} %all-reduce.5.cloned.1.call-done) | copy-start | bytes 25165828
  609.1 12.7 %slice-start.2 = ((s8[8650752]{0:T(1024)(128)(4,1)}), s8[4194304]{0:T(1024)(128)(4,1)S(1)}, s32[]{:S(2)}) async-start(s8[8650752]{0:T(1024)(128)(4,1)} %bitcast.78), calls=%async_computation.4 | async-start | bytes 8388608
  611.0 10.8 %slice-start.3 = ((s8[8650752]{0:T(1024)(128)(4,1)}), s8[4194304]{0:T(1024)(128)(4,1)S(1)}, s32[]{:S(2)}) async-start(s8[8650752]{0:T(1024)(128)(4,1)} %bitcast.78), calls=%async_computation.5 | async-start | bytes 8388608
  611.0 10.8 %slice-start.4 = ((s8[8650752]{0:T(1024)(128)(4,1)}), s8[262144]{0:T(1024)(128)(4,1)S(1)}, s32[]{:S(2)}) async-start(s8[8650752]{0:T(1024)(128)(4,1)} %bitcast.78), calls=%async_computation.6 | async-start | bytes 524288
Sparse Core Ops, SparseCore 0:
  181.7 291.5 all-reduce.4
  493.1 53.6 all-reduce.6
where the time goes:
time: 659 us; the launch traced here: 652 us
  waiting for transfers between devices  346 us (53%)
  other arithmetic  137 us (21%)
  local copies, waits for them, and re-layouts  99.6 us (15%)
  matrix products  44.8 us (7%)
  between operations  16.3 us (2%)
  starting transfers between devices  8.91 us (1%)
    psum x1, waiting for transfers between devices, broadcast(): return lax.psum(jnp.where(mine, array, jnp.zeros_like(array)), axis)  292 us
    psum x1, waiting for transfers between devices, local(): lax.psum((inner_sum(raw_vectors, raw_vectors), inner_sum(raw_vectors, ste...  52.2 us
    add x4, other arithmetic, neighbours(): padded[..., :-2, 1:-1] + padded[..., 2:, 1:-1] + padded[..., 1:-1, :-2]  49.7 us
    another operation x6, other arithmetic, triangle_inverse(): factor = jnp.linalg.cholesky(gram_sums / total_dims)  34.2 us
    unnamed x28, local copies, waits for them, and re-layouts  29.7 us
    slice x5, local copies, waits for them, and re-layouts, with_halo(): lax.slice_in_dim(cells, cells.shape[dim] - width, cells.shape[dim], axis=...  28.5 us
    another operation x3, other arithmetic, triangle_inverse(): return jax.scipy.linalg.solve_triangular(factor, identity_mat, lower=True)  19.7 us
    dot_general x2, matrix products, inner_sum(): jnp.einsum('vcrs,wcrs->vw', left, right, precision=lax.Precision.HIGHEST)  19.6 us
  transfers between devices with their start and end apart: 10, of which 5 were waited for; matrix products, arithmetic and copies ran while one was open for 4% of the time, Pallas kernels for 0%

commit v1 on v0

v1 whole, which is shorter than its diff:
```python
import jax
import jax.numpy as jnp
from jax import lax
from jax.sharding import PartitionSpec as P

time_step = 0.2
coupling = 1.0
kerr_gain = 1.0
streams = 2
chunk_goal = 16
HIGHEST = lax.Precision.HIGHEST
HIGH = lax.Precision.HIGH


def from_before(edge, axis):
    count = lax.axis_size(axis)
    return lax.ppermute(edge, axis, [(i, (i + 1) % count) for i in range(count)])


def from_after(edge, axis):
    count = lax.axis_size(axis)
    return lax.ppermute(edge, axis, [((i + 1) % count, i) for i in range(count)])


def edges(cells, width):
    rows, cols = cells.shape[1], cells.shape[2]
    above = from_before(lax.slice_in_dim(cells, rows - width, rows, axis=1), "gx")
    below = from_after(lax.slice_in_dim(cells, 0, width, axis=1), "gx")
    left = from_before(lax.slice_in_dim(cells, cols - width, cols, axis=2), "gy")
    right = from_after(lax.slice_in_dim(cells, 0, width, axis=2), "gy")
    return above, below, left, right


def neighbour_sum(cells):
    above, below, left, right = edges(cells, 1)
    tall = jnp.concatenate([above, cells, below], axis=1)
    wide = jnp.concatenate([left, cells, right], axis=2)
    return tall[:, :-2] + tall[:, 2:] + wide[:, :, :-2] + wide[:, :, 2:]


def field_rate(cells):
    total = neighbour_sum(cells)
    re_part, im_part = cells[0], cells[1]
    density = re_part * re_part + im_part * im_part
    return jnp.stack(
        [
            -coupling * total[1] - kerr_gain * density * im_part,
            coupling * total[0] + kerr_gain * density * re_part,
        ]
    )


def tangent_rate(base, cells):
    re_part, im_part = base[0][..., None], base[1][..., None]
    total = neighbour_sum(cells)
    re_tan, im_tan = cells[0], cells[1]
    cross_term = 2.0 * re_part * im_part
    weight_re = 3.0 * re_part * re_part + im_part * im_part
    weight_im = re_part * re_part + 3.0 * im_part * im_part
    rate_re = -coupling * total[1] - kerr_gain * (cross_term * re_tan + weight_im * im_tan)
    rate_im = coupling * total[0] + kerr_gain * (weight_re * re_tan + cross_term * im_tan)
    return jnp.stack([rate_re, rate_im])


def add_up(sums, axis):
    count = lax.axis_size(axis)
    if count & (count - 1):
        return lax.psum(sums, axis)
    step = 1
    while step < count:
        sums = sums + lax.ppermute(sums, axis, [(i, i ^ step) for i in range(count)])
        step *= 2
    return sums


def hand_on(sums, place):
    count = lax.axis_size("vec")
    pairs = [(i, i + 1) for i in range(count - 1)]
    held = sums
    for _ in range(count - 1):
        held = jnp.where(place == 0, sums, lax.ppermute(held, "vec", pairs))
    return held


def inverse_pieces(gram):
    half = gram.shape[0] // 2
    eye = jnp.eye(half, dtype=gram.dtype)
    top, side, low = gram[:half, :half], gram[half:, :half], gram[half:, half:]
    (top,) = yield (top,)
    factor = jnp.linalg.cholesky(top)
    (factor,) = yield (factor,)
    first = jax.scipy.linalg.solve_triangular(factor, eye, lower=True)
    (first,) = yield (first,)
    link = jnp.dot(side, first.T, precision=HIGHEST)
    rest = low - jnp.dot(link, link.T, precision=HIGHEST)
    factor = jnp.linalg.cholesky(rest)
    factor, link = yield (factor, link)
    eye = jnp.eye(gram.shape[0] - half, dtype=gram.dtype)
    last = jax.scipy.linalg.solve_triangular(factor, eye, lower=True)
    (last,) = yield (last,)
    corner = -jnp.dot(last, jnp.dot(link, first, precision=HIGHEST), precision=HIGHEST)
    upper = jnp.concatenate([first, jnp.zeros_like(corner.T)], axis=1)
    yield jnp.concatenate([upper, jnp.concatenate([corner, last], axis=1)], axis=0)


def spread_panel(stepped, place, gram):
    count = lax.axis_size("vec")
    parts, rows, cols, vecs = stepped.shape
    lines = parts * rows
    chunks = chunk_goal if lines % (streams * chunk_goal) == 0 else 1
    lanes = streams if lines % streams == 0 else 1
    own = stepped.reshape(lanes, chunks, lines // (lanes * chunks) * cols, vecs)
    pairs = [(i, i + 1) for i in range(count - 1)]
    cross = jnp.zeros((vecs, vecs), jnp.float32)
    got = [[] for _ in range(lanes)]
    turns = chunks + count - 2
    pieces = inverse_pieces(gram)
    state = next(pieces)
    for turn in range(turns):
        if turn >= turns - 8 and isinstance(state, tuple) and got[0]:
            lasts = [blocks[-1] for blocks in got]
            lasts, state = lax.optimization_barrier((lasts, state))
            for blocks, block in zip(got, lasts):
                blocks[-1] = block
            state = pieces.send(state)
        at = turn - (place - 1)
        valid = (place > 0) & (at >= 0) & (at < chunks)
        for lane in range(lanes):
            mine = own[lane, min(turn, chunks - 1)]
            last = got[lane]
            send = jnp.where(place == 0, mine, last[-1]) if last else mine
            block = lax.ppermute(send, "vec", pairs)
            last.append(block)
            here = lax.dynamic_index_in_dim(
                own[lane], jnp.clip(at, 0, chunks - 1), axis=0, keepdims=False
            )
            part = lax.dot_general(block, here, (((0,), (0,)), ((), ())), precision=HIGH)
            cross = cross + jnp.where(valid, part, jnp.zeros_like(part))
    while isinstance(state, tuple):
        state = pieces.send(state)
    first = jnp.maximum(place - 1, 0)
    panel = jnp.stack(
        [lax.dynamic_slice_in_dim(jnp.stack(blocks), first, chunks, axis=0) for blocks in got]
    )
    return jnp.where(place == 0, own, panel), cross, state


def local(field, tangents):
    vecs = tangents.shape[0]
    place = lax.axis_index("vec")
    cells = jnp.transpose(tangents, (1, 2, 3, 0))
    total_dims = cells.size // vecs * lax.axis_size("gx") * lax.axis_size("gy")

    field_half = field + 0.5 * time_step * field_rate(field)
    field_next = field + time_step * field_rate(field_half)
    half = cells + 0.5 * time_step * tangent_rate(field, cells)
    stepped = cells + time_step * tangent_rate(field_half, half)

    flat = stepped.reshape(-1, vecs)
    self_sums = lax.dot_general(flat, flat, (((0,), (0,)), ((), ())), precision=HIGH)
    self_sums = add_up(add_up(self_sums, "gx"), "gy")
    gram = hand_on(self_sums, place) / total_dims
    panel, cross_sums, inverse = spread_panel(stepped, place, gram)
    panel = panel.reshape(-1, vecs)
    cross = add_up(add_up(cross_sums, "gx"), "gy") / total_dims
    coefficients = jnp.dot(inverse, cross, precision=HIGHEST)
    weights = jnp.dot(coefficients.T, inverse, precision=HIGHEST)
    weights = jnp.where(place == 0, -inverse, weights)
    kept = jnp.where(place == 0, jnp.zeros_like(flat), flat)
    change = lax.dot_general(panel, weights, (((1,), (1,)), ((), ())), precision=HIGH)
    result = (kept - change).reshape(cells.shape)
    return field_next, jnp.transpose(result, (3, 0, 1, 2))


def solution(mesh):
    in_specs = (P(None, "gx", "gy"), P("vec", None, "gx", "gy"))
    out_specs = (P(None, "gx", "gy"), P("vec", None, "gx", "gy"))
    return jax.shard_map(local, mesh=mesh, in_specs=in_specs, out_specs=out_specs, check_vma=False)
```

time: 659 us -> 511 us (0.78)
  waiting for transfers between devices: 346 us -> 21.9 us
  starting transfers between devices: 8.91 us -> 144 us
  matrix products: 44.8 us -> 77.3 us
  local copies, waits for them, and re-layouts: 99.6 us -> 129 us
  between operations: 16.3 us -> 2.59 us
  other arithmetic: 137 us -> 128 us
    psum x2 -> x0, waiting for transfers between devices: 344 us -> none  [the longest x1 292 us: broadcast(): return lax.psum(jnp.where(mine, array, jnp.zeros_like(array)), axis)]
    ppermute x8 -> x61, starting transfers between devices: 8.84 us -> 144 us  [the longest x36 118 us: spread_panel(): block = lax.ppermute(send, 'vec', pairs)]
    unnamed x28 -> x174, local copies, waits for them, and re-layouts: 29.7 us -> 82.5 us
    dot_general x5 -> x44, matrix products: 43.5 us -> 75.9 us  [the longest x36 56.3 us: spread_panel(): lax.dot_general(block, here, (((0,), (0,)), ((), ())), precision=HIGH)]
    slice x15 -> x12, local copies, waits for them, and re-layouts: 44.7 us -> 13.6 us  [the longest x1 7.78 us: spread_panel(): own[lane]]
    ppermute x4 -> x0, local copies, waits for them, and re-layouts: 21 us -> none  [the longest x2 10.5 us: with_halo(): lax.ppermute(tail, axis, [(i, (i + 1) % count) for i in range(count)])]
    ppermute x8 -> x61, waiting for transfers between devices: 1.92 us -> 21.9 us  [the longest x36 12.4 us: spread_panel(): block = lax.ppermute(send, 'vec', pairs)]
    dynamic_slice x0 -> x4, local copies, waits for them, and re-layouts: none -> 19.9 us  [spread_panel(): lax.dynamic_slice_in_dim(jnp.stack(blocks), first, chunks, axis=0)]
  transfers between devices with their start and end apart: 10 -> 61, of which waited for: 5 -> 23; matrix products, arithmetic and copies ran while one was open for 4% -> 41% of each run, Pallas kernels for 0% -> 0%
where the time goes in v1:
time: 511 us; the launch traced here: 503 us
  starting transfers between devices  144 us (28%)
  local copies, waits for them, and re-layouts  129 us (25%)
  other arithmetic  128 us (25%)
  matrix products  77.3 us (15%)
  waiting for transfers between devices  21.9 us (4%)
    ppermute x36, starting transfers between devices, spread_panel(): block = lax.ppermute(send, 'vec', pairs)  118 us
    unnamed x174, local copies, waits for them, and re-layouts  82.5 us
    dot_general x36, matrix products, spread_panel(): lax.dot_general(block, here, (((0,), (0,)), ((), ())), precision=HIGH)  56.3 us
    add x4, other arithmetic, neighbour_sum(): return tall[:, :-2] + tall[:, 2:] + wide[:, :, :-2] + wide[:, :, 2:]  32.6 us
    dynamic_slice x4, local copies, waits for them, and re-layouts, spread_panel(): lax.dynamic_slice_in_dim(jnp.stack(blocks), first, chunks, axis=0)  19.9 us
    select_n x34, other arithmetic, spread_panel(): send = jnp.where(place == 0, mine, last[-1]) if last else mine  14.5 us
    another operation x3, other arithmetic, inverse_pieces(): factor = jnp.linalg.cholesky(top)  13.2 us
    another operation x3, other arithmetic, inverse_pieces(): factor = jnp.linalg.cholesky(rest)  12.4 us
  transfers between devices with their start and end apart: 61, of which 23 were waited for; matrix products, arithmetic and copies ran while one was open for 41% of the time, Pallas kernels for 0%

profile of v1, /device:TPU:0, one launch (start us, length us, event | category | flops | bytes accessed | tf_op | source)
XLA Modules:
  0.0 502.9 jit_solution(9178981927926087035)
XLA Ops:
  0.6 9.9 %copy.51 = f32[256,2,32,128]{0,3,2,1:T(8,128)} copy(f32[256,2,32,128]{3,2,1,0:T(8,128)} %param.6) | data formatting | bytes 16777216 | tf_op args[1]
  12.2 2.5 collective-permute-start.2
  18.9 2.4 collective-permute-start.6
  31.0 16.2 %fusion.3 = f32[2,32,128,256]{3,2,1,0:T(8,128)} fusion(f32[2,32,1,256]{3,2,1,0:T(1,128)S(1)} %collective-permute-done.11, f32[2,32,128,256]{3,2,1,0:T(8,128)} %bitcast.365, f32[2,32,1,256]{3,2,1,0:T(1,128)S(1)} %collective-permute-done.10, f32[2,1,128,256]{3,2,1,0:T(8,128)S(1)} %collective-permute-done.9, f32[2,1,128,256]{3,2,1,0:T(8,128)S(1)} %collective-permute-done.8), kind=kLoop, calls=%fused_computation.9 | loop fusion | flops 14680064 | bytes 17432576 | tf_op jit(solution)/shard_map/add | solution.py:38
  47.2 4.9 fusion.9
  54.4 2.8 copy-done.1
  63.1 16.2 %fusion = f32[2,32,128,256]{3,2,1,0:T(8,128)} fusion(f32[2,32,1,256]{3,2,1,0:T(1,128)S(1)} %collective-permute-done.15, f32[2,32,128,256]{3,2,1,0:T(8,128)} %copy-done.1, f32[2,32,1,256]{3,2,1,0:T(1,128)S(1)} %collective-permute-done.14, f32[2,1,128,256]{3,2,1,0:T(8,128)S(1)} %collective-permute-done.13, f32[2,1,128,256]{3,2,1,0:T(8,128)S(1)} %collective-permute-done.12), kind=kLoop, calls=%fused_computation.2 | loop fusion | flops 14680064 | bytes 17432576 | tf_op jit(solution)/shard_map/add | solution.py:38
  79.4 6.8 %fusion.8 = (f32[1,32,128,256]{3,2,1,0:T(8,128)S(1)}, f32[1,32,128,256]{3,2,1,0:T(8,128)S(1)}) fusion(f32[2,32,128,256]{3,2,1,0:T(8,128)} %fusion, f32[2,32,128,256]{3,2,1,0:T(8,128)} %copy-done.1, f32[32,128]{1,0:T(8,128)S(1)} %get-tuple-element.88, f32[32,128]{1,0:T(8,128)S(1)} %get-tuple-element.89, f32[32,128]{1,0:T(8,128)S(1)} %get-tuple-element.90), kind=kLoop, calls=%fused_computation.24 | loop fusion | flops 9437184 | bytes 25214976 | tf_op jit(solution)/shard_map/sub | solution.py:60
  87.9 6.9 %convolution_bitcast_fusion = f32[256,256]{0,1:T(8,128)S(1)} fusion(f32[2,32,128,256]{3,2,1,0:T(8,128)S(1)} %fusion.7), kind=kOutput, calls=%fused_computation.66 | convolution fusion | flops 3221225472 | bytes 8650752 | tf_op jit(solution)/shard_map/dot_general | solution.py:160
  98.8 3.5 collective-permute-start.26
  104.1 3.7 collective-permute-start.16
  107.8 7.8 %fusion.192 = (f32[1,32,128,256]{3,2,1,0:T(8,128)}, f32[1,32,128,256]{3,2,1,0:T(8,128)}) fusion(f32[2,32,128,256]{3,2,1,0:T(8,128)} %copy-done), kind=kLoop, calls=%fused_computation.367 | loop fusion | bytes 16777216 | tf_op jit(solution)/shard_map/slice | solution.py:135
  161.5 3.6 collective-permute-start.27
  171.8 4.5 collective-permute-start.28
  177.5 4.5 collective-permute-start.18
  189.4 3.9 collective-permute-start.19
  196.6 2.3 collective-permute-start.40
  200.0 4.5 collective-permute-start.30
  205.6 4.4 collective-permute-start.20
  216.9 4.5 collective-permute-start.31
  222.5 4.4 collective-permute-start.21
  233.7 4.5 collective-permute-start.32
  239.3 4.4 collective-permute-start.22
  250.5 4.5 collective-permute-start.23
  261.7 3.8 collective-permute-start.24
  270.1 2.6 collective-permute-start.35
  273.7 4.4 collective-permute-start.25
  283.6 12.5 %cholesky.44 = f32[128,128]{1,0:T(8,128)S(1)} custom-call(f32[128,128]{1,0:T(8,128)} %fusion.134), custom_call_target="Cholesky" | custom-call | tf_op jit(solution)/shard_map/jit(cholesky)/cholesky | solution.py:90
  296.8 4.4 collective-permute-start.43
  301.3 2.2 collective-permute-start.42
  312.0 4.4 collective-permute-start.45
  318.1 2.4 collective-permute-start.44
  320.5 9.8 %custom-call.6 = f32[1,128,128]{1,2,0:T(8,128)S(1)} custom-call(f32[1,128,128]{2,1,0:T(8,128)S(1)} %select_bitcast_fusion.1), custom_call_target="InvertDiagBlocksLowerTriangular" | custom-call | tf_op jit(solution)/shard_map/jit(_solve_triangular)/triangular_solve | solution.py:92
  338.5 11.7 %cholesky.55 = f32[128,128]{1,0:T(8,128)S(1)} custom-call(f32[128,128]{1,0:T(8,128)S(1)} %fusion.132), custom_call_target="Cholesky" | custom-call | tf_op jit(solution)/shard_map/jit(cholesky)/cholesky | solution.py:96
  352.7 2.5 collective-permute-start.47
  376.3 10.4 %custom-call.7 = f32[1,128,128]{1,2,0:T(8,128)} custom-call(f32[1,128,128]{2,1,0:T(8,128)S(1)} %select_bitcast_fusion), custom_call_target="InvertDiagBlocksLowerTriangular" | custom-call | tf_op jit(solution)/shard_map/jit(_solve_triangular)/triangular_solve | solution.py:99
  415.6 3.7 collective-permute-start.52
  419.9 4.4 collective-permute-start.56
  428.5 2.2 collective-permute-start.53
  431.7 4.7 collective-permute-start.57
  446.9 4.6 constant_dynamic-slice_fusion.1
  451.4 5.3 %copy.88 = f32[16,256,256]{2,1,0:T(8,128)} copy(f32[16,256,256]{1,2,0:T(8,128)} %constant_dynamic-slice_fusion.1) | data formatting | bytes 8388608 | tf_op jit(solution)/shard_map/dynamic_slice | solution.py:143
  456.8 4.6 constant_dynamic-slice_fusion
  461.4 5.4 %copy.91 = f32[16,256,256]{2,1,0:T(8,128)} copy(f32[16,256,256]{1,2,0:T(8,128)} %constant_dynamic-slice_fusion) | data formatting | bytes 8388608 | tf_op jit(solution)/shard_map/dynamic_slice | solution.py:143
  467.3 7.9 %pad_maximum_fusion.8 = f32[2,16,256,256]{3,2,1,0:T(8,128)} fusion(f32[1,16,256,256]{3,2,1,0:T(8,128)} %bitcast.407, f32[1,16,256,256]{3,2,1,0:T(8,128)} %bitcast.406), kind=kLoop, calls=%fused_computation.19 | loop fusion | flops 2097152 | bytes 16777216 | tf_op jit(solution)/shard_map/stack | solution.py:142
  477.1 6.2 %bitcast_select_fusion = (f32[8192,256]{1,0:T(8,128)S(1)}, f32[8192,256]{1,0:T(8,128)}) fusion(f32[2,16,256,256]{3,2,1,0:T(8,128)} %pad_maximum_fusion.8, f32[2,32,128,256]{3,2,1,0:T(8,128)S(1)} %bitcast.362, pred[]{:T(512)S(6)} %eq.6), kind=kLoop, calls=%fused_computation.20 | loop fusion | flops 4194304 | bytes 33554432 | tf_op jit(solution)/shard_map/jit(_where)/select_n | solution.py:145
  484.6 7.8 %convolution_subtract_fusion = f32[8192,256]{1,0:T(8,128)} fusion(f32[8192,256]{1,0:T(8,128)} %get-tuple-element.43, f32[8192,256]{1,0:T(8,128)S(1)} %get-tuple-element.42, f32[256,256]{0,1:T(8,128)S(1)} %convolution_select_fusion), kind=kOutput, calls=%fused_computation | convolution fusion | flops 3223322624 | bytes 25427968 | tf_op jit(solution)/shard_map/dot_general | solution.py:170
  492.4 10.2 %copy.130 = f32[2,32,128,256]{2,1,0,3:T(8,128)} copy(f32[2,32,128,256]{3,2,1,0:T(8,128)} %bitcast.369) | data formatting | bytes 16777216 | tf_op jit(solution)/shard_map/reshape | solution.py:171
  (391 shorter events, 228.6 us)
Async XLA Ops:
  11.6 19.3 %collective-permute-start.8 = (f32[2,1,128,256]{3,2,1,0:T(8,128)S(1)}, f32[2,1,128,256]{3,2,1,0:T(8,128)S(1)}, u32[]{:S(2)}, u32[]{:S(2)}) collective-permute-start(f32[2,1,128,256]{3,2,1,0:T(8,128)S(1)} %get-tuple-element.80), channel_id=1, source_target_pairs={{0,16},{16,0},{1,17},{17,1},{2,18},{18,2},{3,19},{19,3},{4,20},{20... | collective-permute-start | bytes 786440 | tf_op jit(solution)/shard_map/ppermute | solution.py:17
  53.9 9.3 %collective-permute-start.12 = (f32[2,1,128,256]{3,2,1,0:T(8,128)S(1)}, f32[2,1,128,256]{3,2,1,0:T(8,128)S(1)}, u32[]{:S(2)}, u32[]{:S(2)}) collective-permute-start(f32[2,1,128,256]{3,2,1,0:T(8,128)S(1)} %get-tuple-element.76), channel_id=1, source_target_pairs={{0,16},{16,0},{1,17},{17,1},{2,18},{18,2},{3,19},{19,3},{4,20},{20... | collective-permute-start | bytes 786440 | tf_op jit(solution)/shard_map/ppermute | solution.py:17
  53.9 9.2 %collective-permute-start.13 = (f32[2,1,128,256]{3,2,1,0:T(8,128)S(1)}, f32[2,1,128,256]{3,2,1,0:T(8,128)S(1)}, u32[]{:S(2)}, u32[]{:S(2)}) collective-permute-start(f32[2,1,128,256]{3,2,1,0:T(8,128)S(1)} %get-tuple-element.77), channel_id=1, source_target_pairs={{16,0},{0,16},{17,1},{1,17},{18,2},{2,18},{19,3},{3,19},{20,4},{4,... | collective-permute-start | bytes 786440 | tf_op jit(solution)/shard_map/ppermute | solution.py:22
  98.0 60.6 %collective-permute-start.36 = (f32[256,256]{0,1:T(8,128)S(1)}, f32[256,256]{0,1:T(8,128)}, u32[]{:S(2)}, u32[]{:S(2)}) collective-permute-start(f32[256,256]{0,1:T(8,128)S(1)} %convolution_bitcast_fusion), channel_id=1, source_target_pairs={{0,16},{16,0},{1,17},{17,1},{2,18},{18,2},{3,19},{19,3},{4,20},{20... | collective-permute-start | bytes 786440 | tf_op jit(solution)/shard_map/ppermute | solution.py:71
  98.8 62.6 %collective-permute-start.26 = (f32[256,256]{0,1:T(8,128)}, f32[256,256]{0,1:T(8,128)S(1)}, u32[]{:S(2)}, u32[]{:S(2)}) collective-permute-start(f32[256,256]{0,1:T(8,128)} %bitcast.410), channel_id=1, source_target_pairs={{0,1},{1,2},{2,3},{4,5},{5,6},{6,7},{8,9},{9,10},{10,11},{12,13},{... | collective-permute-start | bytes 786440 | tf_op jit(solution)/shard_map/ppermute | solution.py:132
  104.1 61.0 %collective-permute-start.16 = (f32[256,256]{0,1:T(8,128)}, f32[256,256]{0,1:T(8,128)S(1)}, u32[]{:S(2)}, u32[]{:S(2)}) collective-permute-start(f32[256,256]{0,1:T(8,128)} %bitcast.409), channel_id=1, source_target_pairs={{0,1},{1,2},{2,3},{4,5},{5,6},{6,7},{8,9},{9,10},{10,11},{12,13},{... | collective-permute-start | bytes 786440 | tf_op jit(solution)/shard_map/ppermute | solution.py:132
  159.7 10.2 %collective-permute-start.37 = (f32[256,256]{0,1:T(8,128)S(1)}, f32[256,256]{0,1:T(8,128)S(1)}, u32[]{:S(2)}, u32[]{:S(2)}) collective-permute-start(f32[256,256]{0,1:T(8,128)S(1)} %add.326), channel_id=1, source_target_pairs={{0,4},{4,0},{8,12},{12,8},{1,5},{5,1},{9,13},{13,9},{2,6},{6,2},{1... | collective-permute-start | bytes 786440 | tf_op jit(solution)/shard_map/ppermute | solution.py:71
  161.5 10.3 %collective-permute-start.27 = (f32[256,256]{0,1:T(8,128)S(1)}, f32[256,256]{0,1:T(8,128)S(1)}, u32[]{:S(2)}, u32[]{:S(2)}) collective-permute-start(f32[256,256]{0,1:T(8,128)S(1)} %bitcast_select_fusion.18), channel_id=1, source_target_pairs={{0,1},{1,2},{2,3},{4,5},{5,6},{6,7},{8,9},{9,10},{10,11},{12,13},{... | collective-permute-start | bytes 786440 | tf_op jit(solution)/shard_map/ppermute | solution.py:132
  165.2 12.3 %collective-permute-start.17 = (f32[256,256]{0,1:T(8,128)S(1)}, f32[256,256]{0,1:T(8,128)S(1)}, u32[]{:S(2)}, u32[]{:S(2)}) collective-permute-start(f32[256,256]{0,1:T(8,128)S(1)} %bitcast_select_fusion.35), channel_id=1, source_target_pairs={{0,1},{1,2},{2,3},{4,5},{5,6},{6,7},{8,9},{9,10},{10,11},{12,13},{... | collective-permute-start | bytes 786440 | tf_op jit(solution)/shard_map/ppermute | solution.py:132
  169.9 15.3 %collective-permute-start.38 = (f32[256,256]{0,1:T(8,128)S(1)}, f32[256,256]{0,1:T(8,128)S(1)}, u32[]{:S(2)}, u32[]{:S(2)}) collective-permute-start(f32[256,256]{0,1:T(8,128)S(1)} %add.327), channel_id=1, source_target_pairs={{0,8},{4,12},{8,0},{12,4},{1,9},{5,13},{9,1},{13,5},{2,10},{6,14},... | collective-permute-start | bytes 786440 | tf_op jit(solution)/shard_map/ppermute | solution.py:71
  171.8 15.3 %collective-permute-start.28 = (f32[256,256]{0,1:T(8,128)S(1)}, f32[256,256]{0,1:T(8,128)S(1)}, u32[]{:S(2)}, u32[]{:S(2)}) collective-permute-start(f32[256,256]{0,1:T(8,128)S(1)} %bitcast_select_fusion.19), channel_id=1, source_target_pairs={{0,1},{1,2},{2,3},{4,5},{5,6},{6,7},{8,9},{9,10},{10,11},{12,13},{... | collective-permute-start | bytes 786440 | tf_op jit(solution)/shard_map/ppermute | solution.py:132
  177.5 11.9 %collective-permute-start.18 = (f32[256,256]{0,1:T(8,128)S(1)}, f32[256,256]{0,1:T(8,128)S(1)}, u32[]{:S(2)}, u32[]{:S(2)}) collective-permute-start(f32[256,256]{0,1:T(8,128)S(1)} %bitcast_select_fusion.34), channel_id=1, source_target_pairs={{0,1},{1,2},{2,3},{4,5},{5,6},{6,7},{8,9},{9,10},{10,11},{12,13},{... | collective-permute-start | bytes 786440 | tf_op jit(solution)/shard_map/ppermute | solution.py:132
  185.3 11.3 %collective-permute-start.39 = (f32[256,256]{0,1:T(8,128)S(1)}, f32[256,256]{0,1:T(8,128)S(1)}, u32[]{:S(2)}, u32[]{:S(2)}) collective-permute-start(f32[256,256]{0,1:T(8,128)S(1)} %add.328), channel_id=1, source_target_pairs={{0,1},{1,2},{2,3},{4,5},{5,6},{6,7},{8,9},{9,10},{10,11},{12,13},{... | collective-permute-start | bytes 786440 | tf_op jit(solution)/shard_map/ppermute | solution.py:81
  187.3 12.7 %collective-permute-start.29 = (f32[256,256]{0,1:T(8,128)S(1)}, f32[256,256]{0,1:T(8,128)S(1)}, u32[]{:S(2)}, u32[]{:S(2)}) collective-permute-start(f32[256,256]{0,1:T(8,128)S(1)} %bitcast_select_fusion.20), channel_id=1, source_target_pairs={{0,1},{1,2},{2,3},{4,5},{5,6},{6,7},{8,9},{9,10},{10,11},{12,13},{... | collective-permute-start | bytes 786440 | tf_op jit(solution)/shard_map/ppermute | solution.py:132
  189.4 16.2 %collective-permute-start.19 = (f32[256,256]{0,1:T(8,128)S(1)}, f32[256,256]{0,1:T(8,128)S(1)}, u32[]{:S(2)}, u32[]{:S(2)}) collective-permute-start(f32[256,256]{0,1:T(8,128)S(1)} %bitcast_select_fusion.33), channel_id=1, source_target_pairs={{0,1},{1,2},{2,3},{4,5},{5,6},{6,7},{8,9},{9,10},{10,11},{12,13},{... | collective-permute-start | bytes 786440 | tf_op jit(solution)/shard_map/ppermute | solution.py:132
  196.6 17.4 %collective-permute-start.40 = (f32[256,256]{0,1:T(8,128)S(1)}, f32[256,256]{0,1:T(8,128)S(1)}, u32[]{:S(2)}, u32[]{:S(2)}) collective-permute-start(f32[256,256]{0,1:T(8,128)S(1)} %broadcast_select_fusion.1), channel_id=1, source_target_pairs={{0,1},{1,2},{2,3},{4,5},{5,6},{6,7},{8,9},{9,10},{10,11},{12,13},{... | collective-permute-start | bytes 786440 | tf_op jit(solution)/shard_map/ppermute | solution.py:81
  200.0 16.8 %collective-permute-start.30 = (f32[256,256]{0,1:T(8,128)S(1)}, f32[256,256]{0,1:T(8,128)S(1)}, u32[]{:S(2)}, u32[]{:S(2)}) collective-permute-start(f32[256,256]{0,1:T(8,128)S(1)} %bitcast_select_fusion.21), channel_id=1, source_target_pairs={{0,1},{1,2},{2,3},{4,5},{5,6},{6,7},{8,9},{9,10},{10,11},{12,13},{... | collective-permute-start | bytes 786440 | tf_op jit(solution)/shard_map/ppermute | solution.py:132
  205.6 16.8 %collective-permute-start.20 = (f32[256,256]{0,1:T(8,128)S(1)}, f32[256,256]{0,1:T(8,128)S(1)}, u32[]{:S(2)}, u32[]{:S(2)}) collective-permute-start(f32[256,256]{0,1:T(8,128)S(1)} %bitcast_select_fusion.32), channel_id=1, source_target_pairs={{0,1},{1,2},{2,3},{4,5},{5,6},{6,7},{8,9},{9,10},{10,11},{12,13},{... | collective-permute-start | bytes 786440 | tf_op jit(solution)/shard_map/ppermute | solution.py:132
  214.0 32.9 %collective-permute-start.41 = (f32[256,256]{0,1:T(8,128)S(1)}, f32[256,256]{0,1:T(8,128)S(1)}, u32[]{:S(2)}, u32[]{:S(2)}) collective-permute-start(f32[256,256]{0,1:T(8,128)S(1)} %broadcast_select_fusion), channel_id=1, source_target_pairs={{0,1},{1,2},{2,3},{4,5},{5,6},{6,7},{8,9},{9,10},{10,11},{12,13},{... | collective-permute-start | bytes 786440 | tf_op jit(solution)/shard_map/ppermute | solution.py:81
  216.9 16.8 %collective-permute-start.31 = (f32[256,256]{0,1:T(8,128)S(1)}, f32[256,256]{0,1:T(8,128)S(1)}, u32[]{:S(2)}, u32[]{:S(2)}) collective-permute-start(f32[256,256]{0,1:T(8,128)S(1)} %bitcast_select_fusion.22), channel_id=1, source_target_pairs={{0,1},{1,2},{2,3},{4,5},{5,6},{6,7},{8,9},{9,10},{10,11},{12,13},{... | collective-permute-start | bytes 786440 | tf_op jit(solution)/shard_map/ppermute | solution.py:132
  222.5 16.8 %collective-permute-start.21 = (f32[256,256]{0,1:T(8,128)S(1)}, f32[256,256]{0,1:T(8,128)S(1)}, u32[]{:S(2)}, u32[]{:S(2)}) collective-permute-start(f32[256,256]{0,1:T(8,128)S(1)} %bitcast_select_fusion.31), channel_id=1, source_target_pairs={{0,1},{1,2},{2,3},{4,5},{5,6},{6,7},{8,9},{9,10},{10,11},{12,13},{... | collective-permute-start | bytes 786440 | tf_op jit(solution)/shard_map/ppermute | solution.py:132
  233.7 14.7 %collective-permute-start.32 = (f32[256,256]{0,1:T(8,128)S(1)}, f32[256,256]{0,1:T(8,128)S(1)}, u32[]{:S(2)}, u32[]{:S(2)}) collective-permute-start(f32[256,256]{0,1:T(8,128)S(1)} %bitcast_select_fusion.23), channel_id=1, source_target_pairs={{0,1},{1,2},{2,3},{4,5},{5,6},{6,7},{8,9},{9,10},{10,11},{12,13},{... | collective-permute-start | bytes 786440 | tf_op jit(solution)/shard_map/ppermute | solution.py:132
  239.3 11.1 %collective-permute-start.22 = (f32[256,256]{0,1:T(8,128)S(1)}, f32[256,256]{0,1:T(8,128)S(1)}, u32[]{:S(2)}, u32[]{:S(2)}) collective-permute-start(f32[256,256]{0,1:T(8,128)S(1)} %bitcast_select_fusion.30), channel_id=1, source_target_pairs={{0,1},{1,2},{2,3},{4,5},{5,6},{6,7},{8,9},{9,10},{10,11},{12,13},{... | collective-permute-start | bytes 786440 | tf_op jit(solution)/shard_map/ppermute | solution.py:132
  248.5 11.1 %collective-permute-start.33 = (f32[256,256]{0,1:T(8,128)S(1)}, f32[256,256]{0,1:T(8,128)S(1)}, u32[]{:S(2)}, u32[]{:S(2)}) collective-permute-start(f32[256,256]{0,1:T(8,128)S(1)} %bitcast_select_fusion.24), channel_id=1, source_target_pairs={{0,1},{1,2},{2,3},{4,5},{5,6},{6,7},{8,9},{9,10},{10,11},{12,13},{... | collective-permute-start | bytes 786440 | tf_op jit(solution)/shard_map/ppermute | solution.py:132
  250.5 11.1 %collective-permute-start.23 = (f32[256,256]{0,1:T(8,128)S(1)}, f32[256,256]{0,1:T(8,128)S(1)}, u32[]{:S(2)}, u32[]{:S(2)}) collective-permute-start(f32[256,256]{0,1:T(8,128)S(1)} %bitcast_select_fusion.29), channel_id=1, source_target_pairs={{0,1},{1,2},{2,3},{4,5},{5,6},{6,7},{8,9},{9,10},{10,11},{12,13},{... | collective-permute-start | bytes 786440 | tf_op jit(solution)/shard_map/ppermute | solution.py:132
  259.6 10.5 %collective-permute-start.34 = (f32[256,256]{0,1:T(8,128)S(1)}, f32[256,256]{0,1:T(8,128)S(1)}, u32[]{:S(2)}, u32[]{:S(2)}) collective-permute-start(f32[256,256]{0,1:T(8,128)S(1)} %bitcast_select_fusion.25), channel_id=1, source_target_pairs={{0,1},{1,2},{2,3},{4,5},{5,6},{6,7},{8,9},{9,10},{10,11},{12,13},{... | collective-permute-start | bytes 786440 | tf_op jit(solution)/shard_map/ppermute | solution.py:132
  261.7 12.0 %collective-permute-start.24 = (f32[256,256]{0,1:T(8,128)S(1)}, f32[256,256]{0,1:T(8,128)S(1)}, u32[]{:S(2)}, u32[]{:S(2)}) collective-permute-start(f32[256,256]{0,1:T(8,128)S(1)} %bitcast_select_fusion.28), channel_id=1, source_target_pairs={{0,1},{1,2},{2,3},{4,5},{5,6},{6,7},{8,9},{9,10},{10,11},{12,13},{... | collective-permute-start | bytes 786440 | tf_op jit(solution)/shard_map/ppermute | solution.py:132
  270.1 12.6 %collective-permute-start.35 = (f32[256,256]{0,1:T(8,128)S(1)}, f32[256,256]{0,1:T(8,128)S(1)}, u32[]{:S(2)}, u32[]{:S(2)}) collective-permute-start(f32[256,256]{0,1:T(8,128)S(1)} %bitcast_select_fusion.26), channel_id=1, source_target_pairs={{0,1},{1,2},{2,3},{4,5},{5,6},{6,7},{8,9},{9,10},{10,11},{12,13},{... | collective-permute-start | bytes 786440 | tf_op jit(solution)/shard_map/ppermute | solution.py:132
  273.7 9.1 %collective-permute-start.25 = (f32[256,256]{0,1:T(8,128)S(1)}, f32[256,256]{0,1:T(8,128)S(1)}, u32[]{:S(2)}, u32[]{:S(2)}) collective-permute-start(f32[256,256]{0,1:T(8,128)S(1)} %bitcast_select_fusion.27), channel_id=1, source_target_pairs={{0,1},{1,2},{2,3},{4,5},{5,6},{6,7},{8,9},{9,10},{10,11},{12,13},{... | collective-permute-start | bytes 786440 | tf_op jit(solution)/shard_map/ppermute | solution.py:132
  296.8 12.2 %collective-permute-start.43 = (f32[256,256]{0,1:T(8,128)S(1)}, f32[256,256]{0,1:T(8,128)S(1)}, u32[]{:S(2)}, u32[]{:S(2)}) collective-permute-start(f32[256,256]{0,1:T(8,128)S(1)} %bitcast_select_fusion.16), channel_id=1, source_target_pairs={{0,1},{1,2},{2,3},{4,5},{5,6},{6,7},{8,9},{9,10},{10,11},{12,13},{... | collective-permute-start | bytes 786440 | tf_op jit(solution)/shard_map/ppermute | solution.py:132
  301.3 9.0 %collective-permute-start.42 = (f32[256,256]{0,1:T(8,128)S(1)}, f32[256,256]{0,1:T(8,128)S(1)}, u32[]{:S(2)}, u32[]{:S(2)}) collective-permute-start(f32[256,256]{0,1:T(8,128)S(1)} %bitcast_select_fusion.17), channel_id=1, source_target_pairs={{0,1},{1,2},{2,3},{4,5},{5,6},{6,7},{8,9},{9,10},{10,11},{12,13},{... | collective-permute-start | bytes 786440 | tf_op jit(solution)/shard_map/ppermute | solution.py:132
  312.0 24.1 %collective-permute-start.45 = (f32[256,256]{0,1:T(8,128)}, f32[256,256]{0,1:T(8,128)S(1)}, u32[]{:S(2)}, u32[]{:S(2)}) collective-permute-start(f32[256,256]{0,1:T(8,128)} %bitcast_select_fusion.14), channel_id=1, source_target_pairs={{0,1},{1,2},{2,3},{4,5},{5,6},{6,7},{8,9},{9,10},{10,11},{12,13},{... | collective-permute-start | bytes 786440 | tf_op jit(solution)/shard_map/ppermute | solution.py:132
  318.1 18.1 %collective-permute-start.44 = (f32[256,256]{0,1:T(8,128)}, f32[256,256]{0,1:T(8,128)S(1)}, u32[]{:S(2)}, u32[]{:S(2)}) collective-permute-start(f32[256,256]{0,1:T(8,128)} %bitcast_select_fusion.15), channel_id=1, source_target_pairs={{0,1},{1,2},{2,3},{4,5},{5,6},{6,7},{8,9},{9,10},{10,11},{12,13},{... | collective-permute-start | bytes 786440 | tf_op jit(solution)/shard_map/ppermute | solution.py:132
  352.7 14.5 %collective-permute-start.47 = (f32[256,256]{0,1:T(8,128)}, f32[256,256]{0,1:T(8,128)S(1)}, u32[]{:S(2)}, u32[]{:S(2)}) collective-permute-start(f32[256,256]{0,1:T(8,128)} %bitcast_select_fusion.12), channel_id=1, source_target_pairs={{0,1},{1,2},{2,3},{4,5},{5,6},{6,7},{8,9},{9,10},{10,11},{12,13},{... | collective-permute-start | bytes 786440 | tf_op jit(solution)/shard_map/ppermute | solution.py:132
  356.8 10.3 %collective-permute-start.46 = (f32[256,256]{0,1:T(8,128)}, f32[256,256]{0,1:T(8,128)S(1)}, u32[]{:S(2)}, u32[]{:S(2)}) collective-permute-start(f32[256,256]{0,1:T(8,128)} %bitcast_select_fusion.13), channel_id=1, source_target_pairs={{0,1},{1,2},{2,3},{4,5},{5,6},{6,7},{8,9},{9,10},{10,11},{12,13},{... | collective-permute-start | bytes 786440 | tf_op jit(solution)/shard_map/ppermute | solution.py:132
  369.7 23.7 %collective-permute-start.49 = (f32[256,256]{0,1:T(8,128)}, f32[256,256]{0,1:T(8,128)S(1)}, u32[]{:S(2)}, u32[]{:S(2)}) collective-permute-start(f32[256,256]{0,1:T(8,128)} %bitcast_select_fusion.10), channel_id=1, source_target_pairs={{0,1},{1,2},{2,3},{4,5},{5,6},{6,7},{8,9},{9,10},{10,11},{12,13},{... | collective-permute-start | bytes 786440 | tf_op jit(solution)/shard_map/ppermute | solution.py:132
  373.3 20.1 %collective-permute-start.48 = (f32[256,256]{0,1:T(8,128)}, f32[256,256]{0,1:T(8,128)S(1)}, u32[]{:S(2)}, u32[]{:S(2)}) collective-permute-start(f32[256,256]{0,1:T(8,128)} %bitcast_select_fusion.11), channel_id=1, source_target_pairs={{0,1},{1,2},{2,3},{4,5},{5,6},{6,7},{8,9},{9,10},{10,11},{12,13},{... | collective-permute-start | bytes 786440 | tf_op jit(solution)/shard_map/ppermute | solution.py:132
  395.2 12.1 %collective-permute-start.50 = (f32[256,256]{0,1:T(8,128)}, f32[256,256]{0,1:T(8,128)S(1)}, u32[]{:S(2)}, u32[]{:S(2)}) collective-permute-start(f32[256,256]{0,1:T(8,128)} %bitcast_select_fusion.9), channel_id=1, source_target_pairs={{0,1},{1,2},{2,3},{4,5},{5,6},{6,7},{8,9},{9,10},{10,11},{12,13},{... | collective-permute-start | bytes 786440 | tf_op jit(solution)/shard_map/ppermute | solution.py:132
  398.8 10.5 %collective-permute-start.54 = (f32[256,256]{0,1:T(8,128)}, f32[256,256]{0,1:T(8,128)S(1)}, u32[]{:S(2)}, u32[]{:S(2)}) collective-permute-start(f32[256,256]{0,1:T(8,128)} %bitcast_select_fusion.5), channel_id=1, source_target_pairs={{0,1},{1,2},{2,3},{4,5},{5,6},{6,7},{8,9},{9,10},{10,11},{12,13},{... | collective-permute-start | bytes 786440 | tf_op jit(solution)/shard_map/ppermute | solution.py:132
  407.3 8.1 %collective-permute-start.51 = (f32[256,256]{0,1:T(8,128)S(1)}, f32[256,256]{0,1:T(8,128)S(1)}, u32[]{:S(2)}, u32[]{:S(2)}) collective-permute-start(f32[256,256]{0,1:T(8,128)S(1)} %bitcast_select_fusion.8), channel_id=1, source_target_pairs={{0,1},{1,2},{2,3},{4,5},{5,6},{6,7},{8,9},{9,10},{10,11},{12,13},{... | collective-permute-start | bytes 786440 | tf_op jit(solution)/shard_map/ppermute | solution.py:132
  409.3 10.6 %collective-permute-start.55 = (f32[256,256]{0,1:T(8,128)S(1)}, f32[256,256]{0,1:T(8,128)S(1)}, u32[]{:S(2)}, u32[]{:S(2)}) collective-permute-start(f32[256,256]{0,1:T(8,128)S(1)} %bitcast_select_fusion.4), channel_id=1, source_target_pairs={{0,1},{1,2},{2,3},{4,5},{5,6},{6,7},{8,9},{9,10},{10,11},{12,13},{... | collective-permute-start | bytes 786440 | tf_op jit(solution)/shard_map/ppermute | solution.py:132
  415.6 12.8 %collective-permute-start.52 = (f32[256,256]{0,1:T(8,128)S(1)}, f32[256,256]{0,1:T(8,128)S(1)}, u32[]{:S(2)}, u32[]{:S(2)}) collective-permute-start(f32[256,256]{0,1:T(8,128)S(1)} %bitcast_select_fusion.7), channel_id=1, source_target_pairs={{0,1},{1,2},{2,3},{4,5},{5,6},{6,7},{8,9},{9,10},{10,11},{12,13},{... | collective-permute-start | bytes 786440 | tf_op jit(solution)/shard_map/ppermute | solution.py:132
  419.9 11.7 %collective-permute-start.56 = (f32[256,256]{0,1:T(8,128)S(1)}, f32[256,256]{0,1:T(8,128)S(1)}, u32[]{:S(2)}, u32[]{:S(2)}) collective-permute-start(f32[256,256]{0,1:T(8,128)S(1)} %bitcast_select_fusion.3), channel_id=1, source_target_pairs={{0,1},{1,2},{2,3},{4,5},{5,6},{6,7},{8,9},{9,10},{10,11},{12,13},{... | collective-permute-start | bytes 786440 | tf_op jit(solution)/shard_map/ppermute | solution.py:132
  428.5 12.0 %collective-permute-start.53 = (f32[256,256]{0,1:T(8,128)S(1)}, f32[256,256]{0,1:T(8,128)S(1)}, u32[]{:S(2)}, u32[]{:S(2)}) collective-permute-start(f32[256,256]{0,1:T(8,128)S(1)} %bitcast_select_fusion.6), channel_id=1, source_target_pairs={{0,1},{1,2},{2,3},{4,5},{5,6},{6,7},{8,9},{9,10},{10,11},{12,13},{... | collective-permute-start | bytes 786440 | tf_op jit(solution)/shard_map/ppermute | solution.py:132
  431.7 10.2 %collective-permute-start.57 = (f32[256,256]{0,1:T(8,128)S(1)}, f32[256,256]{0,1:T(8,128)S(1)}, u32[]{:S(2)}, u32[]{:S(2)}) collective-permute-start(f32[256,256]{0,1:T(8,128)S(1)} %bitcast_select_fusion.2), channel_id=1, source_target_pairs={{0,1},{1,2},{2,3},{4,5},{5,6},{6,7},{8,9},{9,10},{10,11},{12,13},{... | collective-permute-start | bytes 786440 | tf_op jit(solution)/shard_map/ppermute | solution.py:132
  445.4 21.4 %collective-permute-start.58 = (f32[256,256]{0,1:T(8,128)S(1)}, f32[256,256]{0,1:T(8,128)S(1)}, u32[]{:S(2)}, u32[]{:S(2)}) collective-permute-start(f32[256,256]{0,1:T(8,128)S(1)} %fusion.44), channel_id=1, source_target_pairs={{0,16},{16,0},{1,17},{17,1},{2,18},{18,2},{3,19},{19,3},{4,20},{20... | collective-permute-start | bytes 786440 | tf_op jit(solution)/shard_map/ppermute | solution.py:71
  466.8 8.8 %collective-permute-start.59 = (f32[256,256]{0,1:T(8,128)S(1)}, f32[256,256]{0,1:T(8,128)S(1)}, u32[]{:S(2)}, u32[]{:S(2)}) collective-permute-start(f32[256,256]{0,1:T(8,128)S(1)} %add.364), channel_id=1, source_target_pairs={{0,4},{4,0},{8,12},{12,8},{1,5},{5,1},{9,13},{13,9},{2,6},{6,2},{1... | collective-permute-start | bytes 786440 | tf_op jit(solution)/shard_map/ppermute | solution.py:71
  475.6 8.0 %collective-permute-start.60 = (f32[256,256]{0,1:T(8,128)S(1)}, f32[256,256]{0,1:T(8,128)S(1)}, u32[]{:S(2)}, u32[]{:S(2)}) collective-permute-start(f32[256,256]{0,1:T(8,128)S(1)} %add.365), channel_id=1, source_target_pairs={{0,8},{4,12},{8,0},{12,4},{1,9},{5,13},{9,1},{13,5},{2,10},{6,14},... | collective-permute-start | bytes 786440 | tf_op jit(solution)/shard_map/ppermute | solution.py:71
  (67 other events, 1400.7 us)

commit v2 on v1

--- a/solution.py
+++ b/solution.py
@@ -82,7 +82,12 @@
     return held
 
 
-def inverse_pieces(gram):
+def inverse_pieces(sums, place, total_dims):
+    for axis in ("gx", "gy"):
+        (sums,) = yield (sums,)
+        sums = add_up(sums, axis)
+    (sums,) = yield (sums,)
+    gram = hand_on(sums, place) / total_dims
     half = gram.shape[0] // 2
     eye = jnp.eye(half, dtype=gram.dtype)
     top, side, low = gram[:half, :half], gram[half:, :half], gram[half:, half:]
@@ -103,7 +108,7 @@
     yield jnp.concatenate([upper, jnp.concatenate([corner, last], axis=1)], axis=0)
 
 
-def spread_panel(stepped, place, gram):
+def spread_panel(stepped, place, sums, total_dims):
     count = lax.axis_size("vec")
     parts, rows, cols, vecs = stepped.shape
     lines = parts * rows
@@ -114,10 +119,10 @@
     cross = jnp.zeros((vecs, vecs), jnp.float32)
     got = [[] for _ in range(lanes)]
     turns = chunks + count - 2
-    pieces = inverse_pieces(gram)
+    pieces = inverse_pieces(sums, place, total_dims)
     state = next(pieces)
     for turn in range(turns):
-        if turn >= turns - 8 and isinstance(state, tuple) and got[0]:
+        if turn % 2 == 0 and isinstance(state, tuple) and got[0]:
             lasts = [blocks[-1] for blocks in got]
             lasts, state = lax.optimization_barrier((lasts, state))
             for blocks, block in zip(got, lasts):
@@ -158,9 +163,7 @@
 
     flat = stepped.reshape(-1, vecs)
     self_sums = lax.dot_general(flat, flat, (((0,), (0,)), ((), ())), precision=HIGH)
-    self_sums = add_up(add_up(self_sums, "gx"), "gy")
-    gram = hand_on(self_sums, place) / total_dims
-    panel, cross_sums, inverse = spread_panel(stepped, place, gram)
+    panel, cross_sums, inverse = spread_panel(stepped, place, self_sums, total_dims)
     panel = panel.reshape(-1, vecs)
     cross = add_up(add_up(cross_sums, "gx"), "gy") / total_dims
     coefficients = jnp.dot(inverse, cross, precision=HIGHEST)

time: 511 us -> 516 us (level)
  matrix products: 77.3 us -> 86.9 us
  starting transfers between devices: 144 us -> 138 us
    dot_general x36, matrix products: 56.3 us -> 66.7 us  [spread_panel(): lax.dot_general(block, here, (((0,), (0,)), ((), ())), precision=HIGH)]
    ppermute x36, starting transfers between devices: 118 us -> 110 us  [spread_panel(): block = lax.ppermute(send, 'vec', pairs)]
    unnamed x174 -> x168, local copies, waits for them, and re-layouts: 82.5 us -> 82.7 us
  transfers between devices with their start and end apart: 61 -> 61, of which waited for: 23 -> 21; matrix products, arithmetic and copies ran while one was open for 41% -> 42% of each run, Pallas kernels for 0% -> 0%
where the time goes in v2:
time: 516 us; the launch traced here: 508 us
  starting transfers between devices  138 us (27%)
  other arithmetic  131 us (25%)
  local copies, waits for them, and re-layouts  127 us (25%)
  matrix products  86.9 us (17%)
  waiting for transfers between devices  22.8 us (4%)
    ppermute x36, starting transfers between devices, spread_panel(): block = lax.ppermute(send, 'vec', pairs)  110 us
    unnamed x168, local copies, waits for them, and re-layouts  82.7 us
    dot_general x36, matrix products, spread_panel(): lax.dot_general(block, here, (((0,), (0,)), ((), ())), precision=HIGH)  66.7 us
    add x4, other arithmetic, neighbour_sum(): return tall[:, :-2] + tall[:, 2:] + wide[:, :, :-2] + wide[:, :, 2:]  32.6 us
    dynamic_slice x4, local copies, waits for them, and re-layouts, spread_panel(): lax.dynamic_slice_in_dim(jnp.stack(blocks), first, chunks, axis=0)  19.9 us
    select_n x34, other arithmetic, spread_panel(): send = jnp.where(place == 0, mine, last[-1]) if last else mine  19.5 us
    another operation x3, other arithmetic, inverse_pieces(): factor = jnp.linalg.cholesky(top)  13.2 us
    another operation x3, other arithmetic, inverse_pieces(): factor = jnp.linalg.cholesky(rest)  12.4 us
  transfers between devices with their start and end apart: 61, of which 21 were waited for; matrix products, arithmetic and copies ran while one was open for 42% of the time, Pallas kernels for 0%

profile of v2, /device:TPU:0, one launch (start us, length us, event | category | flops | bytes accessed | tf_op | source)
XLA Modules:
  0.0 508.0 jit_solution(6884863211769909312)
XLA Ops:
  0.6 9.9 %copy.51 = f32[256,2,32,128]{0,3,2,1:T(8,128)} copy(f32[256,2,32,128]{3,2,1,0:T(8,128)} %param.6) | data formatting | bytes 16777216 | tf_op args[1]
  12.2 2.5 collective-permute-start.2
  18.9 2.4 collective-permute-start.6
  31.0 16.2 %fusion.3 = f32[2,32,128,256]{3,2,1,0:T(8,128)} fusion(f32[2,32,1,256]{3,2,1,0:T(1,128)S(1)} %collective-permute-done.11, f32[2,32,128,256]{3,2,1,0:T(8,128)} %bitcast.365, f32[2,32,1,256]{3,2,1,0:T(1,128)S(1)} %collective-permute-done.10, f32[2,1,128,256]{3,2,1,0:T(8,128)S(1)} %collective-permute-done.9, f32[2,1,128,256]{3,2,1,0:T(8,128)S(1)} %collective-permute-done.8), kind=kLoop, calls=%fused_computation.9 | loop fusion | flops 14680064 | bytes 17432576 | tf_op jit(solution)/shard_map/add | solution.py:38
  47.2 4.9 fusion.9
  54.4 2.8 copy-done.1
  63.2 16.2 %fusion = f32[2,32,128,256]{3,2,1,0:T(8,128)} fusion(f32[2,32,1,256]{3,2,1,0:T(1,128)S(1)} %collective-permute-done.15, f32[2,32,128,256]{3,2,1,0:T(8,128)} %copy-done.1, f32[2,32,1,256]{3,2,1,0:T(1,128)S(1)} %collective-permute-done.14, f32[2,1,128,256]{3,2,1,0:T(8,128)S(1)} %collective-permute-done.13, f32[2,1,128,256]{3,2,1,0:T(8,128)S(1)} %collective-permute-done.12), kind=kLoop, calls=%fused_computation.2 | loop fusion | flops 14680064 | bytes 17432576 | tf_op jit(solution)/shard_map/add | solution.py:38
  79.4 6.8 %fusion.8 = (f32[1,32,128,256]{3,2,1,0:T(8,128)S(1)}, f32[1,32,128,256]{3,2,1,0:T(8,128)S(1)}) fusion(f32[2,32,128,256]{3,2,1,0:T(8,128)} %fusion, f32[2,32,128,256]{3,2,1,0:T(8,128)} %copy-done.1, f32[32,128]{1,0:T(8,128)S(1)} %get-tuple-element.106, f32[32,128]{1,0:T(8,128)S(1)} %get-tuple-element.107, f32[32,128]{1,0:T(8,128)S(1)} %get-tuple-element.108), kind=kLoop, calls=%fused_computation.24 | loop fusion | flops 9437184 | bytes 25214976 | tf_op jit(solution)/shard_map/sub | solution.py:60
  87.9 6.9 %convolution_bitcast_fusion = f32[256,256]{1,0:T(8,128)S(1)} fusion(f32[2,32,128,256]{3,2,1,0:T(8,128)S(1)} %fusion.7), kind=kOutput, calls=%fused_computation.66 | convolution fusion | flops 3221225472 | bytes 8650752 | tf_op jit(solution)/shard_map/dot_general | solution.py:165
  94.8 3.9 fusion.192
  101.2 3.5 collective-permute-start.18
  105.5 3.9 collective-permute-start.16
  109.4 3.9 fusion.193
  157.1 3.5 collective-permute-start.19
  166.3 2.8 collective-permute-done.17
  169.4 4.5 collective-permute-start.22
  174.9 2.2 collective-permute-start.20
  181.3 3.8 collective-permute-start.23
  186.2 4.5 collective-permute-start.21
  198.2 4.5 collective-permute-start.27
  202.8 2.3 collective-permute-start.25
  210.7 3.4 collective-permute-start.28
  215.1 4.5 collective-permute-start.26
  225.3 3.7 collective-permute-start.35
  241.4 4.4 collective-permute-start.34
  247.0 4.4 collective-permute-start.32
  257.1 2.4 collective-permute-start.37
  261.6 2.3 collective-permute-done.32
  268.3 12.5 %cholesky.44 = f32[128,128]{1,0:T(8,128)S(1)} custom-call(f32[128,128]{1,0:T(8,128)} %fusion.134), custom_call_target="Cholesky" | custom-call | tf_op jit(solution)/shard_map/jit(cholesky)/cholesky | solution.py:95
  281.8 4.4 collective-permute-start.40
  293.3 4.4 collective-permute-start.41
  297.9 4.4 collective-permute-start.39
  309.6 2.8 collective-permute-start.44
  321.0 9.8 %custom-call.6 = f32[1,128,128]{1,2,0:T(8,128)S(1)} custom-call(f32[1,128,128]{2,1,0:T(8,128)S(1)} %select_bitcast_fusion.1), custom_call_target="InvertDiagBlocksLowerTriangular" | custom-call | tf_op jit(solution)/shard_map/jit(_solve_triangular)/triangular_solve | solution.py:97
  345.3 11.7 %cholesky.55 = f32[128,128]{1,0:T(8,128)S(1)} custom-call(f32[128,128]{1,0:T(8,128)S(1)} %fusion.132), custom_call_target="Cholesky" | custom-call | tf_op jit(solution)/shard_map/jit(cholesky)/cholesky | solution.py:101
  359.3 3.0 collective-permute-start.48
  389.4 2.7 collective-permute-start.52
  400.7 9.8 %custom-call.7 = f32[1,128,128]{1,2,0:T(8,128)S(1)} custom-call(f32[1,128,128]{2,1,0:T(8,128)S(1)} %select_bitcast_fusion), custom_call_target="InvertDiagBlocksLowerTriangular" | custom-call | tf_op jit(solution)/shard_map/jit(_solve_triangular)/triangular_solve | solution.py:104
  421.7 4.5 collective-permute-start.54
  438.0 2.8 collective-permute-start.57
  451.4 4.5 constant_dynamic-slice_fusion.1
  455.9 5.3 %copy.90 = f32[16,256,256]{2,1,0:T(8,128)} copy(f32[16,256,256]{1,2,0:T(8,128)} %constant_dynamic-slice_fusion.1) | data formatting | bytes 8388608 | tf_op jit(solution)/shard_map/dynamic_slice | solution.py:148
  461.2 4.6 constant_dynamic-slice_fusion
  465.8 5.4 %copy.91 = f32[16,256,256]{2,1,0:T(8,128)} copy(f32[16,256,256]{1,2,0:T(8,128)} %constant_dynamic-slice_fusion) | data formatting | bytes 8388608 | tf_op jit(solution)/shard_map/dynamic_slice | solution.py:148
  472.2 7.8 %pad_maximum_fusion.8 = f32[2,16,256,256]{3,2,1,0:T(8,128)} fusion(f32[1,16,256,256]{3,2,1,0:T(8,128)} %bitcast.407, f32[1,16,256,256]{3,2,1,0:T(8,128)} %bitcast.406), kind=kLoop, calls=%fused_computation.19 | loop fusion | flops 2097152 | bytes 16777216 | tf_op jit(solution)/shard_map/stack | solution.py:147
  481.3 6.2 %bitcast_select_fusion = (f32[8192,256]{1,0:T(8,128)S(1)}, f32[8192,256]{1,0:T(8,128)}) fusion(f32[2,16,256,256]{3,2,1,0:T(8,128)} %pad_maximum_fusion.8, f32[2,32,128,256]{3,2,1,0:T(8,128)S(1)} %bitcast.362, pred[]{:T(512)S(6)} %eq.6), kind=kLoop, calls=%fused_computation.20 | loop fusion | flops 4194304 | bytes 33554432 | tf_op jit(solution)/shard_map/jit(_where)/select_n | solution.py:150
  489.5 7.9 %convolution_subtract_fusion = f32[8192,256]{1,0:T(8,128)} fusion(f32[8192,256]{1,0:T(8,128)} %get-tuple-element.61, f32[8192,256]{1,0:T(8,128)S(1)} %get-tuple-element.60, f32[256,256]{0,1:T(8,128)S(1)} %convolution_select_fusion), kind=kOutput, calls=%fused_computation | convolution fusion | flops 3223322624 | bytes 25427968 | tf_op jit(solution)/shard_map/dot_general | solution.py:173
  497.3 10.2 %copy.130 = f32[2,32,128,256]{2,1,0,3:T(8,128)} copy(f32[2,32,128,256]{3,2,1,0:T(8,128)} %bitcast.369) | data formatting | bytes 16777216 | tf_op jit(solution)/shard_map/reshape | solution.py:174
  (386 shorter events, 243.5 us)
Async XLA Ops:
  11.6 19.3 %collective-permute-start.8 = (f32[2,1,128,256]{3,2,1,0:T(8,128)S(1)}, f32[2,1,128,256]{3,2,1,0:T(8,128)S(1)}, u32[]{:S(2)}, u32[]{:S(2)}) collective-permute-start(f32[2,1,128,256]{3,2,1,0:T(8,128)S(1)} %get-tuple-element.98), channel_id=1, source_target_pairs={{0,16},{16,0},{1,17},{17,1},{2,18},{18,2},{3,19},{19,3},{4,20},{20... | collective-permute-start | bytes 786440 | tf_op jit(solution)/shard_map/ppermute | solution.py:17
  53.8 9.3 %collective-permute-start.12 = (f32[2,1,128,256]{3,2,1,0:T(8,128)S(1)}, f32[2,1,128,256]{3,2,1,0:T(8,128)S(1)}, u32[]{:S(2)}, u32[]{:S(2)}) collective-permute-start(f32[2,1,128,256]{3,2,1,0:T(8,128)S(1)} %get-tuple-element.94), channel_id=1, source_target_pairs={{0,16},{16,0},{1,17},{17,1},{2,18},{18,2},{3,19},{19,3},{4,20},{20... | collective-permute-start | bytes 786440 | tf_op jit(solution)/shard_map/ppermute | solution.py:17
  53.9 9.3 %collective-permute-start.13 = (f32[2,1,128,256]{3,2,1,0:T(8,128)S(1)}, f32[2,1,128,256]{3,2,1,0:T(8,128)S(1)}, u32[]{:S(2)}, u32[]{:S(2)}) collective-permute-start(f32[2,1,128,256]{3,2,1,0:T(8,128)S(1)} %get-tuple-element.95), channel_id=1, source_target_pairs={{16,0},{0,16},{17,1},{1,17},{18,2},{2,18},{19,3},{3,19},{20,4},{4,... | collective-permute-start | bytes 786440 | tf_op jit(solution)/shard_map/ppermute | solution.py:22
  101.2 54.9 %collective-permute-start.18 = (f32[256,256]{0,1:T(8,128)}, f32[256,256]{0,1:T(8,128)S(1)}, u32[]{:S(2)}, u32[]{:S(2)}) collective-permute-start(f32[256,256]{0,1:T(8,128)} %bitcast.11), channel_id=1, source_target_pairs={{0,1},{1,2},{2,3},{4,5},{5,6},{6,7},{8,9},{9,10},{10,11},{12,13},{... | collective-permute-start | bytes 786440 | tf_op jit(solution)/shard_map/ppermute | solution.py:137
  105.5 55.1 %collective-permute-start.16 = (f32[256,256]{0,1:T(8,128)}, f32[256,256]{0,1:T(8,128)S(1)}, u32[]{:S(2)}, u32[]{:S(2)}) collective-permute-start(f32[256,256]{0,1:T(8,128)} %bitcast.7), channel_id=1, source_target_pairs={{0,1},{1,2},{2,3},{4,5},{5,6},{6,7},{8,9},{9,10},{10,11},{12,13},{... | collective-permute-start | bytes 786440 | tf_op jit(solution)/shard_map/ppermute | solution.py:137
  157.1 9.2 %collective-permute-start.19 = (f32[256,256]{0,1:T(8,128)S(1)}, f32[256,256]{0,1:T(8,128)S(1)}, u32[]{:S(2)}, u32[]{:S(2)}) collective-permute-start(f32[256,256]{0,1:T(8,128)S(1)} %bitcast_select_fusion.34), channel_id=1, source_target_pairs={{0,1},{1,2},{2,3},{4,5},{5,6},{6,7},{8,9},{9,10},{10,11},{12,13},{... | collective-permute-start | bytes 786440 | tf_op jit(solution)/shard_map/ppermute | solution.py:137
  160.7 8.5 %collective-permute-start.17 = (f32[256,256]{0,1:T(8,128)S(1)}, f32[256,256]{0,1:T(8,128)S(1)}, u32[]{:S(2)}, u32[]{:S(2)}) collective-permute-start(f32[256,256]{0,1:T(8,128)S(1)} %bitcast_select_fusion.35), channel_id=1, source_target_pairs={{0,1},{1,2},{2,3},{4,5},{5,6},{6,7},{8,9},{9,10},{10,11},{12,13},{... | collective-permute-start | bytes 786440 | tf_op jit(solution)/shard_map/ppermute | solution.py:137
  169.3 24.9 %collective-permute-start.24 = (f32[256,256]{0,1:T(8,128)S(1)}, f32[256,256]{0,1:T(8,128)S(1)}, u32[]{:S(2)}, u32[]{:S(2)}) collective-permute-start(f32[256,256]{0,1:T(8,128)S(1)} %copy.62), channel_id=1, source_target_pairs={{0,16},{16,0},{1,17},{17,1},{2,18},{18,2},{3,19},{19,3},{4,20},{20... | collective-permute-start | bytes 786440 | tf_op jit(solution)/shard_map/ppermute | solution.py:71
  169.4 11.9 %collective-permute-start.22 = (f32[256,256]{0,1:T(8,128)S(1)}, f32[256,256]{0,1:T(8,128)S(1)}, u32[]{:S(2)}, u32[]{:S(2)}) collective-permute-start(f32[256,256]{0,1:T(8,128)S(1)} %bitcast_select_fusion.30), channel_id=1, source_target_pairs={{0,1},{1,2},{2,3},{4,5},{5,6},{6,7},{8,9},{9,10},{10,11},{12,13},{... | collective-permute-start | bytes 786440 | tf_op jit(solution)/shard_map/ppermute | solution.py:137
  174.9 11.2 %collective-permute-start.20 = (f32[256,256]{0,1:T(8,128)S(1)}, f32[256,256]{0,1:T(8,128)S(1)}, u32[]{:S(2)}, u32[]{:S(2)}) collective-permute-start(f32[256,256]{0,1:T(8,128)S(1)} %bitcast_select_fusion.33), channel_id=1, source_target_pairs={{0,1},{1,2},{2,3},{4,5},{5,6},{6,7},{8,9},{9,10},{10,11},{12,13},{... | collective-permute-start | bytes 786440 | tf_op jit(solution)/shard_map/ppermute | solution.py:137
  181.3 13.6 %collective-permute-start.23 = (f32[256,256]{0,1:T(8,128)S(1)}, f32[256,256]{0,1:T(8,128)S(1)}, u32[]{:S(2)}, u32[]{:S(2)}) collective-permute-start(f32[256,256]{0,1:T(8,128)S(1)} %bitcast_select_fusion.31), channel_id=1, source_target_pairs={{0,1},{1,2},{2,3},{4,5},{5,6},{6,7},{8,9},{9,10},{10,11},{12,13},{... | collective-permute-start | bytes 786440 | tf_op jit(solution)/shard_map/ppermute | solution.py:137
  186.2 10.8 %collective-permute-start.21 = (f32[256,256]{0,1:T(8,128)S(1)}, f32[256,256]{0,1:T(8,128)S(1)}, u32[]{:S(2)}, u32[]{:S(2)}) collective-permute-start(f32[256,256]{0,1:T(8,128)S(1)} %bitcast_select_fusion.32), channel_id=1, source_target_pairs={{0,1},{1,2},{2,3},{4,5},{5,6},{6,7},{8,9},{9,10},{10,11},{12,13},{... | collective-permute-start | bytes 786440 | tf_op jit(solution)/shard_map/ppermute | solution.py:137
  197.0 12.4 %collective-permute-start.29 = (f32[256,256]{0,1:T(8,128)S(1)}, f32[256,256]{0,1:T(8,128)S(1)}, u32[]{:S(2)}, u32[]{:S(2)}) collective-permute-start(f32[256,256]{0,1:T(8,128)S(1)} %add.326), channel_id=1, source_target_pairs={{0,4},{4,0},{8,12},{12,8},{1,5},{5,1},{9,13},{13,9},{2,6},{6,2},{1... | collective-permute-start | bytes 786440 | tf_op jit(solution)/shard_map/ppermute | solution.py:71
  198.2 12.4 %collective-permute-start.27 = (f32[256,256]{0,1:T(8,128)S(1)}, f32[256,256]{0,1:T(8,128)S(1)}, u32[]{:S(2)}, u32[]{:S(2)}) collective-permute-start(f32[256,256]{0,1:T(8,128)S(1)} %bitcast_select_fusion.26), channel_id=1, source_target_pairs={{0,1},{1,2},{2,3},{4,5},{5,6},{6,7},{8,9},{9,10},{10,11},{12,13},{... | collective-permute-start | bytes 786440 | tf_op jit(solution)/shard_map/ppermute | solution.py:137
  202.8 12.3 %collective-permute-start.25 = (f32[256,256]{0,1:T(8,128)S(1)}, f32[256,256]{0,1:T(8,128)S(1)}, u32[]{:S(2)}, u32[]{:S(2)}) collective-permute-start(f32[256,256]{0,1:T(8,128)S(1)} %bitcast_select_fusion.29), channel_id=1, source_target_pairs={{0,1},{1,2},{2,3},{4,5},{5,6},{6,7},{8,9},{9,10},{10,11},{12,13},{... | collective-permute-start | bytes 786440 | tf_op jit(solution)/shard_map/ppermute | solution.py:137
  209.5 15.8 %collective-permute-start.30 = (f32[256,256]{0,1:T(8,128)S(1)}, f32[256,256]{0,1:T(8,128)S(1)}, u32[]{:S(2)}, u32[]{:S(2)}) collective-permute-start(f32[256,256]{0,1:T(8,128)S(1)} %add.327), channel_id=1, source_target_pairs={{0,8},{4,12},{8,0},{12,4},{1,9},{5,13},{9,1},{13,5},{2,10},{6,14},... | collective-permute-start | bytes 786440 | tf_op jit(solution)/shard_map/ppermute | solution.py:71
  210.7 14.6 %collective-permute-start.28 = (f32[256,256]{0,1:T(8,128)S(1)}, f32[256,256]{0,1:T(8,128)S(1)}, u32[]{:S(2)}, u32[]{:S(2)}) collective-permute-start(f32[256,256]{0,1:T(8,128)S(1)} %bitcast_select_fusion.27), channel_id=1, source_target_pairs={{0,1},{1,2},{2,3},{4,5},{5,6},{6,7},{8,9},{9,10},{10,11},{12,13},{... | collective-permute-start | bytes 786440 | tf_op jit(solution)/shard_map/ppermute | solution.py:137
  215.1 10.2 %collective-permute-start.26 = (f32[256,256]{0,1:T(8,128)S(1)}, f32[256,256]{0,1:T(8,128)S(1)}, u32[]{:S(2)}, u32[]{:S(2)}) collective-permute-start(f32[256,256]{0,1:T(8,128)S(1)} %bitcast_select_fusion.28), channel_id=1, source_target_pairs={{0,1},{1,2},{2,3},{4,5},{5,6},{6,7},{8,9},{9,10},{10,11},{12,13},{... | collective-permute-start | bytes 786440 | tf_op jit(solution)/shard_map/ppermute | solution.py:137
  225.3 13.8 %collective-permute-start.35 = (f32[256,256]{0,1:T(8,128)S(1)}, f32[256,256]{0,1:T(8,128)S(1)}, u32[]{:S(2)}, u32[]{:S(2)}) collective-permute-start(f32[256,256]{0,1:T(8,128)S(1)} %add.328), channel_id=1, source_target_pairs={{0,1},{1,2},{2,3},{4,5},{5,6},{6,7},{8,9},{9,10},{10,11},{12,13},{... | collective-permute-start | bytes 786440 | tf_op jit(solution)/shard_map/ppermute | solution.py:81
  229.1 12.3 %collective-permute-start.33 = (f32[256,256]{0,1:T(8,128)S(1)}, f32[256,256]{0,1:T(8,128)S(1)}, u32[]{:S(2)}, u32[]{:S(2)}) collective-permute-start(f32[256,256]{0,1:T(8,128)S(1)} %bitcast_select_fusion.22), channel_id=1, source_target_pairs={{0,1},{1,2},{2,3},{4,5},{5,6},{6,7},{8,9},{9,10},{10,11},{12,13},{... | collective-permute-start | bytes 786440 | tf_op jit(solution)/shard_map/ppermute | solution.py:137
  231.3 15.6 %collective-permute-start.31 = (f32[256,256]{0,1:T(8,128)S(1)}, f32[256,256]{0,1:T(8,128)S(1)}, u32[]{:S(2)}, u32[]{:S(2)}) collective-permute-start(f32[256,256]{0,1:T(8,128)S(1)} %bitcast_select_fusion.25), channel_id=1, source_target_pairs={{0,1},{1,2},{2,3},{4,5},{5,6},{6,7},{8,9},{9,10},{10,11},{12,13},{... | collective-permute-start | bytes 786440 | tf_op jit(solution)/shard_map/ppermute | solution.py:137
  239.1 18.0 %collective-permute-start.36 = (f32[256,256]{0,1:T(8,128)S(1)}, f32[256,256]{0,1:T(8,128)S(1)}, u32[]{:S(2)}, u32[]{:S(2)}) collective-permute-start(f32[256,256]{0,1:T(8,128)S(1)} %broadcast_select_fusion.1), channel_id=1, source_target_pairs={{0,1},{1,2},{2,3},{4,5},{5,6},{6,7},{8,9},{9,10},{10,11},{12,13},{... | collective-permute-start | bytes 786440 | tf_op jit(solution)/shard_map/ppermute | solution.py:81
  241.4 18.1 %collective-permute-start.34 = (f32[256,256]{0,1:T(8,128)S(1)}, f32[256,256]{0,1:T(8,128)S(1)}, u32[]{:S(2)}, u32[]{:S(2)}) collective-permute-start(f32[256,256]{0,1:T(8,128)S(1)} %bitcast_select_fusion.23), channel_id=1, source_target_pairs={{0,1},{1,2},{2,3},{4,5},{5,6},{6,7},{8,9},{9,10},{10,11},{12,13},{... | collective-permute-start | bytes 786440 | tf_op jit(solution)/shard_map/ppermute | solution.py:137
  247.0 16.8 %collective-permute-start.32 = (f32[256,256]{0,1:T(8,128)S(1)}, f32[256,256]{0,1:T(8,128)S(1)}, u32[]{:S(2)}, u32[]{:S(2)}) collective-permute-start(f32[256,256]{0,1:T(8,128)S(1)} %bitcast_select_fusion.24), channel_id=1, source_target_pairs={{0,1},{1,2},{2,3},{4,5},{5,6},{6,7},{8,9},{9,10},{10,11},{12,13},{... | collective-permute-start | bytes 786440 | tf_op jit(solution)/shard_map/ppermute | solution.py:137
  257.1 9.6 %collective-permute-start.37 = (f32[256,256]{0,1:T(8,128)S(1)}, f32[256,256]{0,1:T(8,128)S(1)}, u32[]{:S(2)}, u32[]{:S(2)}) collective-permute-start(f32[256,256]{0,1:T(8,128)S(1)} %broadcast_select_fusion), channel_id=1, source_target_pairs={{0,1},{1,2},{2,3},{4,5},{5,6},{6,7},{8,9},{9,10},{10,11},{12,13},{... | collective-permute-start | bytes 786440 | tf_op jit(solution)/shard_map/ppermute | solution.py:81
  281.8 10.4 %collective-permute-start.40 = (f32[256,256]{0,1:T(8,128)S(1)}, f32[256,256]{0,1:T(8,128)S(1)}, u32[]{:S(2)}, u32[]{:S(2)}) collective-permute-start(f32[256,256]{0,1:T(8,128)S(1)} %bitcast_select_fusion.18), channel_id=1, source_target_pairs={{0,1},{1,2},{2,3},{4,5},{5,6},{6,7},{8,9},{9,10},{10,11},{12,13},{... | collective-permute-start | bytes 786440 | tf_op jit(solution)/shard_map/ppermute | solution.py:137
  287.2 10.6 %collective-permute-start.38 = (f32[256,256]{0,1:T(8,128)S(1)}, f32[256,256]{0,1:T(8,128)S(1)}, u32[]{:S(2)}, u32[]{:S(2)}) collective-permute-start(f32[256,256]{0,1:T(8,128)S(1)} %bitcast_select_fusion.21), channel_id=1, source_target_pairs={{0,1},{1,2},{2,3},{4,5},{5,6},{6,7},{8,9},{9,10},{10,11},{12,13},{... | collective-permute-start | bytes 786440 | tf_op jit(solution)/shard_map/ppermute | solution.py:137
  293.3 14.6 %collective-permute-start.41 = (f32[256,256]{0,1:T(8,128)S(1)}, f32[256,256]{0,1:T(8,128)S(1)}, u32[]{:S(2)}, u32[]{:S(2)}) collective-permute-start(f32[256,256]{0,1:T(8,128)S(1)} %bitcast_select_fusion.19), channel_id=1, source_target_pairs={{0,1},{1,2},{2,3},{4,5},{5,6},{6,7},{8,9},{9,10},{10,11},{12,13},{... | collective-permute-start | bytes 786440 | tf_op jit(solution)/shard_map/ppermute | solution.py:137
  297.9 10.0 %collective-permute-start.39 = (f32[256,256]{0,1:T(8,128)S(1)}, f32[256,256]{0,1:T(8,128)S(1)}, u32[]{:S(2)}, u32[]{:S(2)}) collective-permute-start(f32[256,256]{0,1:T(8,128)S(1)} %bitcast_select_fusion.20), channel_id=1, source_target_pairs={{0,1},{1,2},{2,3},{4,5},{5,6},{6,7},{8,9},{9,10},{10,11},{12,13},{... | collective-permute-start | bytes 786440 | tf_op jit(solution)/shard_map/ppermute | solution.py:137
  309.6 21.5 %collective-permute-start.44 = (f32[256,256]{0,1:T(8,128)}, f32[256,256]{0,1:T(8,128)S(1)}, u32[]{:S(2)}, u32[]{:S(2)}) collective-permute-start(f32[256,256]{0,1:T(8,128)} %bitcast_select_fusion.14), channel_id=1, source_target_pairs={{0,1},{1,2},{2,3},{4,5},{5,6},{6,7},{8,9},{9,10},{10,11},{12,13},{... | collective-permute-start | bytes 786440 | tf_op jit(solution)/shard_map/ppermute | solution.py:137
  313.2 21.1 %collective-permute-start.42 = (f32[256,256]{0,1:T(8,128)}, f32[256,256]{0,1:T(8,128)S(1)}, u32[]{:S(2)}, u32[]{:S(2)}) collective-permute-start(f32[256,256]{0,1:T(8,128)} %bitcast_select_fusion.17), channel_id=1, source_target_pairs={{0,1},{1,2},{2,3},{4,5},{5,6},{6,7},{8,9},{9,10},{10,11},{12,13},{... | collective-permute-start | bytes 786440 | tf_op jit(solution)/shard_map/ppermute | solution.py:137
  332.1 10.9 %collective-permute-start.45 = (f32[256,256]{0,1:T(8,128)S(1)}, f32[256,256]{0,1:T(8,128)S(1)}, u32[]{:S(2)}, u32[]{:S(2)}) collective-permute-start(f32[256,256]{0,1:T(8,128)S(1)} %bitcast_select_fusion.15), channel_id=1, source_target_pairs={{0,1},{1,2},{2,3},{4,5},{5,6},{6,7},{8,9},{9,10},{10,11},{12,13},{... | collective-permute-start | bytes 786440 | tf_op jit(solution)/shard_map/ppermute | solution.py:137
  335.3 7.7 %collective-permute-start.43 = (f32[256,256]{0,1:T(8,128)S(1)}, f32[256,256]{0,1:T(8,128)S(1)}, u32[]{:S(2)}, u32[]{:S(2)}) collective-permute-start(f32[256,256]{0,1:T(8,128)S(1)} %bitcast_select_fusion.16), channel_id=1, source_target_pairs={{0,1},{1,2},{2,3},{4,5},{5,6},{6,7},{8,9},{9,10},{10,11},{12,13},{... | collective-permute-start | bytes 786440 | tf_op jit(solution)/shard_map/ppermute | solution.py:137
  359.3 15.9 %collective-permute-start.48 = (f32[256,256]{0,1:T(8,128)}, f32[256,256]{0,1:T(8,128)S(1)}, u32[]{:S(2)}, u32[]{:S(2)}) collective-permute-start(f32[256,256]{0,1:T(8,128)} %bitcast_select_fusion.10), channel_id=1, source_target_pairs={{0,1},{1,2},{2,3},{4,5},{5,6},{6,7},{8,9},{9,10},{10,11},{12,13},{... | collective-permute-start | bytes 786440 | tf_op jit(solution)/shard_map/ppermute | solution.py:137
  364.0 14.4 %collective-permute-start.46 = (f32[256,256]{0,1:T(8,128)}, f32[256,256]{0,1:T(8,128)S(1)}, u32[]{:S(2)}, u32[]{:S(2)}) collective-permute-start(f32[256,256]{0,1:T(8,128)} %bitcast_select_fusion.13), channel_id=1, source_target_pairs={{0,1},{1,2},{2,3},{4,5},{5,6},{6,7},{8,9},{9,10},{10,11},{12,13},{... | collective-permute-start | bytes 786440 | tf_op jit(solution)/shard_map/ppermute | solution.py:137
  376.3 10.7 %collective-permute-start.49 = (f32[256,256]{0,1:T(8,128)S(1)}, f32[256,256]{0,1:T(8,128)S(1)}, u32[]{:S(2)}, u32[]{:S(2)}) collective-permute-start(f32[256,256]{0,1:T(8,128)S(1)} %bitcast_select_fusion.11), channel_id=1, source_target_pairs={{0,1},{1,2},{2,3},{4,5},{5,6},{6,7},{8,9},{9,10},{10,11},{12,13},{... | collective-permute-start | bytes 786440 | tf_op jit(solution)/shard_map/ppermute | solution.py:137
  379.5 7.5 %collective-permute-start.47 = (f32[256,256]{0,1:T(8,128)S(1)}, f32[256,256]{0,1:T(8,128)S(1)}, u32[]{:S(2)}, u32[]{:S(2)}) collective-permute-start(f32[256,256]{0,1:T(8,128)S(1)} %bitcast_select_fusion.12), channel_id=1, source_target_pairs={{0,1},{1,2},{2,3},{4,5},{5,6},{6,7},{8,9},{9,10},{10,11},{12,13},{... | collective-permute-start | bytes 786440 | tf_op jit(solution)/shard_map/ppermute | solution.py:137
  389.4 21.3 %collective-permute-start.52 = (f32[256,256]{0,1:T(8,128)}, f32[256,256]{0,1:T(8,128)S(1)}, u32[]{:S(2)}, u32[]{:S(2)}) collective-permute-start(f32[256,256]{0,1:T(8,128)} %bitcast_select_fusion.2), channel_id=1, source_target_pairs={{0,1},{1,2},{2,3},{4,5},{5,6},{6,7},{8,9},{9,10},{10,11},{12,13},{... | collective-permute-start | bytes 786440 | tf_op jit(solution)/shard_map/ppermute | solution.py:137
  393.2 19.8 %collective-permute-start.50 = (f32[256,256]{0,1:T(8,128)S(1)}, f32[256,256]{0,1:T(8,128)S(1)}, u32[]{:S(2)}, u32[]{:S(2)}) collective-permute-start(f32[256,256]{0,1:T(8,128)S(1)} %bitcast_select_fusion.9), channel_id=1, source_target_pairs={{0,1},{1,2},{2,3},{4,5},{5,6},{6,7},{8,9},{9,10},{10,11},{12,13},{... | collective-permute-start | bytes 786440 | tf_op jit(solution)/shard_map/ppermute | solution.py:137
  410.8 10.0 %collective-permute-start.53 = (f32[256,256]{0,1:T(8,128)S(1)}, f32[256,256]{0,1:T(8,128)S(1)}, u32[]{:S(2)}, u32[]{:S(2)}) collective-permute-start(f32[256,256]{0,1:T(8,128)S(1)} %bitcast_select_fusion.5), channel_id=1, source_target_pairs={{0,1},{1,2},{2,3},{4,5},{5,6},{6,7},{8,9},{9,10},{10,11},{12,13},{... | collective-permute-start | bytes 786440 | tf_op jit(solution)/shard_map/ppermute | solution.py:137
  413.1 7.9 %collective-permute-start.51 = (f32[256,256]{0,1:T(8,128)S(1)}, f32[256,256]{0,1:T(8,128)S(1)}, u32[]{:S(2)}, u32[]{:S(2)}) collective-permute-start(f32[256,256]{0,1:T(8,128)S(1)} %bitcast_select_fusion.8), channel_id=1, source_target_pairs={{0,1},{1,2},{2,3},{4,5},{5,6},{6,7},{8,9},{9,10},{10,11},{12,13},{... | collective-permute-start | bytes 786440 | tf_op jit(solution)/shard_map/ppermute | solution.py:137
  421.7 14.0 %collective-permute-start.54 = (f32[256,256]{0,1:T(8,128)}, f32[256,256]{0,1:T(8,128)S(1)}, u32[]{:S(2)}, u32[]{:S(2)}) collective-permute-start(f32[256,256]{0,1:T(8,128)} %bitcast_select_fusion.7), channel_id=1, source_target_pairs={{0,1},{1,2},{2,3},{4,5},{5,6},{6,7},{8,9},{9,10},{10,11},{12,13},{... | collective-permute-start | bytes 786440 | tf_op jit(solution)/shard_map/ppermute | solution.py:137
  427.0 11.0 %collective-permute-start.56 = (f32[256,256]{0,1:T(8,128)}, f32[256,256]{0,1:T(8,128)S(1)}, u32[]{:S(2)}, u32[]{:S(2)}) collective-permute-start(f32[256,256]{0,1:T(8,128)} %bitcast_select_fusion.4), channel_id=1, source_target_pairs={{0,1},{1,2},{2,3},{4,5},{5,6},{6,7},{8,9},{9,10},{10,11},{12,13},{... | collective-permute-start | bytes 786440 | tf_op jit(solution)/shard_map/ppermute | solution.py:137
  435.7 9.2 %collective-permute-start.55 = (f32[256,256]{0,1:T(8,128)S(1)}, f32[256,256]{0,1:T(8,128)S(1)}, u32[]{:S(2)}, u32[]{:S(2)}) collective-permute-start(f32[256,256]{0,1:T(8,128)S(1)} %bitcast_select_fusion.6), channel_id=1, source_target_pairs={{0,1},{1,2},{2,3},{4,5},{5,6},{6,7},{8,9},{9,10},{10,11},{12,13},{... | collective-permute-start | bytes 786440 | tf_op jit(solution)/shard_map/ppermute | solution.py:137
  438.0 8.3 %collective-permute-start.57 = (f32[256,256]{0,1:T(8,128)S(1)}, f32[256,256]{0,1:T(8,128)S(1)}, u32[]{:S(2)}, u32[]{:S(2)}) collective-permute-start(f32[256,256]{0,1:T(8,128)S(1)} %bitcast_select_fusion.3), channel_id=1, source_target_pairs={{0,1},{1,2},{2,3},{4,5},{5,6},{6,7},{8,9},{9,10},{10,11},{12,13},{... | collective-permute-start | bytes 786440 | tf_op jit(solution)/shard_map/ppermute | solution.py:137
  449.8 21.4 %collective-permute-start.58 = (f32[256,256]{0,1:T(8,128)S(1)}, f32[256,256]{0,1:T(8,128)S(1)}, u32[]{:S(2)}, u32[]{:S(2)}) collective-permute-start(f32[256,256]{0,1:T(8,128)S(1)} %fusion.44), channel_id=1, source_target_pairs={{0,16},{16,0},{1,17},{17,1},{2,18},{18,2},{3,19},{19,3},{4,20},{20... | collective-permute-start | bytes 786440 | tf_op jit(solution)/shard_map/ppermute | solution.py:71
  471.3 8.8 %collective-permute-start.59 = (f32[256,256]{0,1:T(8,128)S(1)}, f32[256,256]{0,1:T(8,128)S(1)}, u32[]{:S(2)}, u32[]{:S(2)}) collective-permute-start(f32[256,256]{0,1:T(8,128)S(1)} %add.364), channel_id=1, source_target_pairs={{0,4},{4,0},{8,12},{12,8},{1,5},{5,1},{9,13},{13,9},{2,6},{6,2},{1... | collective-permute-start | bytes 786440 | tf_op jit(solution)/shard_map/ppermute | solution.py:71
  480.1 8.5 %collective-permute-start.60 = (f32[256,256]{0,1:T(8,128)S(1)}, f32[256,256]{0,1:T(8,128)S(1)}, u32[]{:S(2)}, u32[]{:S(2)}) collective-permute-start(f32[256,256]{0,1:T(8,128)S(1)} %add.365), channel_id=1, source_target_pairs={{0,8},{4,12},{8,0},{12,4},{1,9},{5,13},{9,1},{13,5},{2,10},{6,14},... | collective-permute-start | bytes 786440 | tf_op jit(solution)/shard_map/ppermute | solution.py:71
  (64 other events, 963.8 us)

commit v3 on v1

--- a/solution.py
+++ b/solution.py
@@ -82,28 +82,7 @@
     return held
 
 
-def inverse_pieces(gram):
-    half = gram.shape[0] // 2
-    eye = jnp.eye(half, dtype=gram.dtype)
-    top, side, low = gram[:half, :half], gram[half:, :half], gram[half:, half:]
-    (top,) = yield (top,)
-    factor = jnp.linalg.cholesky(top)
-    (factor,) = yield (factor,)
-    first = jax.scipy.linalg.solve_triangular(factor, eye, lower=True)
-    (first,) = yield (first,)
-    link = jnp.dot(side, first.T, precision=HIGHEST)
-    rest = low - jnp.dot(link, link.T, precision=HIGHEST)
-    factor = jnp.linalg.cholesky(rest)
-    factor, link = yield (factor, link)
-    eye = jnp.eye(gram.shape[0] - half, dtype=gram.dtype)
-    last = jax.scipy.linalg.solve_triangular(factor, eye, lower=True)
-    (last,) = yield (last,)
-    corner = -jnp.dot(last, jnp.dot(link, first, precision=HIGHEST), precision=HIGHEST)
-    upper = jnp.concatenate([first, jnp.zeros_like(corner.T)], axis=1)
-    yield jnp.concatenate([upper, jnp.concatenate([corner, last], axis=1)], axis=0)
-
-
-def spread_panel(stepped, place, gram):
+def spread_panel(stepped, place):
     count = lax.axis_size("vec")
     parts, rows, cols, vecs = stepped.shape
     lines = parts * rows
@@ -113,16 +92,7 @@
     pairs = [(i, i + 1) for i in range(count - 1)]
     cross = jnp.zeros((vecs, vecs), jnp.float32)
     got = [[] for _ in range(lanes)]
-    turns = chunks + count - 2
-    pieces = inverse_pieces(gram)
-    state = next(pieces)
-    for turn in range(turns):
-        if turn >= turns - 8 and isinstance(state, tuple) and got[0]:
-            lasts = [blocks[-1] for blocks in got]
-            lasts, state = lax.optimization_barrier((lasts, state))
-            for blocks, block in zip(got, lasts):
-                blocks[-1] = block
-            state = pieces.send(state)
+    for turn in range(chunks + count - 2):
         at = turn - (place - 1)
         valid = (place > 0) & (at >= 0) & (at < chunks)
         for lane in range(lanes):
@@ -136,13 +106,11 @@
             )
             part = lax.dot_general(block, here, (((0,), (0,)), ((), ())), precision=HIGH)
             cross = cross + jnp.where(valid, part, jnp.zeros_like(part))
-    while isinstance(state, tuple):
-        state = pieces.send(state)
     first = jnp.maximum(place - 1, 0)
     panel = jnp.stack(
         [lax.dynamic_slice_in_dim(jnp.stack(blocks), first, chunks, axis=0) for blocks in got]
     )
-    return jnp.where(place == 0, own, panel), cross, state
+    return jnp.where(place == 0, own, panel), cross
 
 
 def local(field, tangents):
@@ -160,7 +128,12 @@
     self_sums = lax.dot_general(flat, flat, (((0,), (0,)), ((), ())), precision=HIGH)
     self_sums = add_up(add_up(self_sums, "gx"), "gy")
     gram = hand_on(self_sums, place) / total_dims
-    panel, cross_sums, inverse = spread_panel(stepped, place, gram)
+    factor = jnp.linalg.cholesky(gram)
+    inverse = jax.scipy.linalg.solve_triangular(
+        factor, jnp.eye(vecs, dtype=jnp.float32), lower=True
+    )
+
+    panel, cross_sums = spread_panel(stepped, place)
     panel = panel.reshape(-1, vecs)
     cross = add_up(add_up(cross_sums, "gx"), "gy") / total_dims
     coefficients = jnp.dot(inverse, cross, precision=HIGHEST)

time: 511 us -> 501 us (0.980)
  matrix products: 77.3 us -> 50.9 us
  starting transfers between devices: 144 us -> 153 us
    dot_general x36, matrix products: 56.3 us -> 33 us  [spread_panel(): lax.dot_general(block, here, (((0,), (0,)), ((), ())), precision=HIGH)]
    ppermute x36, starting transfers between devices: 118 us -> 128 us  [spread_panel(): block = lax.ppermute(send, 'vec', pairs)]
    another operation x10 -> x9, other arithmetic: 46.7 us -> 54.5 us  [the longest x6 34 us: local(): factor = jnp.linalg.cholesky(gram)]
    another operation x0 -> x19, local copies, waits for them, and re-layouts: none -> 5.78 us
    unnamed x174 -> x145, local copies, waits for them, and re-layouts: 82.5 us -> 81.9 us
  transfers between devices with their start and end apart: 61 -> 61, of which waited for: 23 -> 24; matrix products, arithmetic and copies ran while one was open for 41% -> 45% of each run, Pallas kernels for 0% -> 0%
where the time goes in v3:
time: 501 us; the launch traced here: 494 us
  starting transfers between devices  153 us (31%)
  local copies, waits for them, and re-layouts  133 us (27%)
  other arithmetic  130 us (26%)
  matrix products  50.9 us (10%)
  waiting for transfers between devices  23.1 us (5%)
    ppermute x36, starting transfers between devices, spread_panel(): block = lax.ppermute(send, 'vec', pairs)  128 us
    unnamed x145, local copies, waits for them, and re-layouts  81.9 us
    another operation x6, other arithmetic, local(): factor = jnp.linalg.cholesky(gram)  34 us
    dot_general x36, matrix products, spread_panel(): lax.dot_general(block, here, (((0,), (0,)), ((), ())), precision=HIGH)  33 us
    add x4, other arithmetic, neighbour_sum(): return tall[:, :-2] + tall[:, 2:] + wide[:, :, :-2] + wide[:, :, 2:]  32.6 us
    another operation x3, other arithmetic, local(): jax.scipy.linalg.solve_triangular(factor, jnp.eye(vecs, dtype=jnp.float32...  20.5 us
    dynamic_slice x4, local copies, waits for them, and re-layouts, spread_panel(): lax.dynamic_slice_in_dim(jnp.stack(blocks), first, chunks, axis=0)  19.9 us
    ppermute x36, waiting for transfers between devices, spread_panel(): block = lax.ppermute(send, 'vec', pairs)  14.2 us
  transfers between devices with their start and end apart: 61, of which 24 were waited for; matrix products, arithmetic and copies ran while one was open for 45% of the time, Pallas kernels for 0%

profile of v3, /device:TPU:0, one launch (start us, length us, event | category | flops | bytes accessed | tf_op | source)
XLA Modules:
  0.0 493.8 jit_solution(6469641937712216172)
XLA Ops:
  0.6 9.9 %copy.53 = f32[256,2,32,128]{0,3,2,1:T(8,128)} copy(f32[256,2,32,128]{3,2,1,0:T(8,128)} %param.3) | data formatting | bytes 16777216 | tf_op args[1]
  31.0 16.2 %fusion.3 = f32[2,32,128,256]{3,2,1,0:T(8,128)} fusion(f32[2,32,1,256]{3,2,1,0:T(1,128)S(1)} %collective-permute-done.11, f32[2,32,128,256]{3,2,1,0:T(8,128)} %bitcast.369, f32[2,32,1,256]{3,2,1,0:T(1,128)S(1)} %collective-permute-done.10, f32[2,1,128,256]{3,2,1,0:T(8,128)S(1)} %collective-permute-done.9, f32[2,1,128,256]{3,2,1,0:T(8,128)S(1)} %collective-permute-done.8), kind=kLoop, calls=%fused_computation.11 | loop fusion | flops 14680064 | bytes 17432576 | tf_op jit(solution)/shard_map/add | solution.py:38
  47.2 4.9 fusion.9
  63.1 16.2 %fusion = f32[2,32,128,256]{3,2,1,0:T(8,128)} fusion(f32[2,32,1,256]{3,2,1,0:T(1,128)S(1)} %collective-permute-done.15, f32[2,32,128,256]{3,2,1,0:T(8,128)} %copy-done.1, f32[2,32,1,256]{3,2,1,0:T(1,128)S(1)} %collective-permute-done.14, f32[2,1,128,256]{3,2,1,0:T(8,128)S(1)} %collective-permute-done.13, f32[2,1,128,256]{3,2,1,0:T(8,128)S(1)} %collective-permute-done.12), kind=kLoop, calls=%fused_computation.4 | loop fusion | flops 14680064 | bytes 17432576 | tf_op jit(solution)/shard_map/add | solution.py:38
  79.3 6.8 %fusion.8 = (f32[1,32,128,256]{3,2,1,0:T(8,128)S(1)}, f32[1,32,128,256]{3,2,1,0:T(8,128)S(1)}) fusion(f32[2,32,128,256]{3,2,1,0:T(8,128)} %fusion, f32[2,32,128,256]{3,2,1,0:T(8,128)} %copy-done.1, f32[32,128]{1,0:T(8,128)S(1)} %get-tuple-element.82, f32[32,128]{1,0:T(8,128)S(1)} %get-tuple-element.83, f32[32,128]{1,0:T(8,128)S(1)} %get-tuple-element.84), kind=kLoop, calls=%fused_computation.26 | loop fusion | flops 9437184 | bytes 25214976 | tf_op jit(solution)/shard_map/sub | solution.py:60
  87.8 6.9 %convolution_bitcast_fusion = f32[256,256]{0,1:T(8,128)S(1)} fusion(f32[2,32,128,256]{3,2,1,0:T(8,128)S(1)} %fusion.7), kind=kOutput, calls=%fused_computation.68 | convolution fusion | flops 3221225472 | bytes 8650752 | tf_op jit(solution)/shard_map/dot_general | solution.py:128
  98.7 3.5 collective-permute-start.16
  103.0 3.7 collective-permute-start.34
  106.7 7.7 %fusion.183 = (f32[1,32,128,256]{3,2,1,0:T(8,128)}, f32[1,32,128,256]{3,2,1,0:T(8,128)}) fusion(f32[2,32,128,256]{3,2,1,0:T(8,128)} %copy-done), kind=kLoop, calls=%fused_computation.363 | loop fusion | bytes 16777216 | tf_op jit(solution)/shard_map/slice | solution.py:105
  160.1 3.6 collective-permute-start.17
  170.5 4.5 collective-permute-start.18
  176.1 4.5 collective-permute-start.36
  199.2 4.4 collective-permute-start.20
  204.8 4.4 collective-permute-start.38
  217.5 3.6 collective-permute-start.21
  222.3 4.8 collective-permute-start.39
  232.9 11.7 %cholesky.50 = f32[128,128]{1,0:T(8,128)S(1)} custom-call(f32[128,128]{1,0:T(8,128)S(1)} %cholesky.118), custom_call_target="Cholesky" | custom-call | tf_op jit(solution)/shard_map/jit(cholesky)/cholesky | solution.py:131
  244.7 9.8 %custom-call.15 = f32[1,128,128]{1,2,0:T(8,128)S(1)} custom-call(f32[1,128,128]{2,1,0:T(8,128)S(1)} %get-tuple-element.77), custom_call_target="InvertDiagBlocksLowerTriangular" | custom-call | tf_op jit(solution)/shard_map/jit(cholesky)/cholesky | solution.py:131
  255.0 11.7 %cholesky.105 = f32[128,128]{1,0:T(8,128)S(1)} custom-call(f32[128,128]{1,0:T(8,128)S(1)} %convolution_subtract_fusion.2), custom_call_target="Cholesky" | custom-call | tf_op jit(solution)/shard_map/jit(cholesky)/cholesky | solution.py:131
  269.1 5.5 %while.1 = (s32[]{:T(128)}, f32[256,256]{0,1:T(8,128)S(1)}, s32[2,2]{1,0:T(2,128)S(1)}, f32[2,128,128]{2,1,0:T(8,128)}, s32[]{:T(128)}) while((s32[]{:T(128)}, f32[256,256]{0,1:T(8,128)S(1)}, s32[2,2]{1,0:T(2,128)S(1)}, f32[2,128,128]{2,1,0:T(8,128)}, s32[]{:T(128)}) %tuple.75), condition=%wide.while_cond, body=%wide.while_body.sunk | while | flops 2 | bytes 393829 | solution.py:132
  274.6 20.5 %custom-call.16 = f32[2,128,128]{1,2,0:T(8,128)S(1)} custom-call(f32[2,128,128]{2,1,0:T(8,128)} %get-tuple-element.9), custom_call_target="InvertDiagBlocksLowerTriangular" | custom-call | tf_op jit(solution)/shard_map/jit(_solve_triangular)/triangular_solve | solution.py:132
  325.2 3.0 collective-permute-start.42
  332.5 3.0 collective-permute-start.25
  335.8 4.4 collective-permute-start.43
  342.5 4.2 collective-permute-start.26
  347.9 4.4 collective-permute-start.44
  354.6 3.3 collective-permute-start.27
  359.1 4.4 collective-permute-start.45
  365.8 3.3 collective-permute-start.28
  370.4 4.4 collective-permute-start.46
  377.1 3.3 collective-permute-start.29
  381.6 4.6 collective-permute-start.47
  388.5 3.1 collective-permute-start.30
  392.8 4.4 collective-permute-start.48
  399.5 3.3 collective-permute-start.31
  404.1 4.4 collective-permute-start.49
  410.8 3.5 collective-permute-start.32
  415.3 4.4 collective-permute-start.50
  422.0 3.5 collective-permute-start.33
  426.7 4.4 collective-permute-start.51
  437.8 4.5 constant_dynamic-slice_fusion.2
  442.4 5.4 %copy.70 = f32[16,256,256]{2,1,0:T(8,128)} copy(f32[16,256,256]{1,2,0:T(8,128)} %constant_dynamic-slice_fusion.2) | data formatting | bytes 8388608 | tf_op jit(solution)/shard_map/dynamic_slice | solution.py:111
  447.7 4.6 constant_dynamic-slice_fusion.1
  452.3 5.4 %copy.87 = f32[16,256,256]{2,1,0:T(8,128)} copy(f32[16,256,256]{1,2,0:T(8,128)} %constant_dynamic-slice_fusion.1) | data formatting | bytes 8388608 | tf_op jit(solution)/shard_map/dynamic_slice | solution.py:111
  458.2 7.9 %pad_maximum_fusion.8 = f32[2,16,256,256]{3,2,1,0:T(8,128)} fusion(f32[1,16,256,256]{3,2,1,0:T(8,128)} %bitcast.411, f32[1,16,256,256]{3,2,1,0:T(8,128)} %bitcast.410), kind=kLoop, calls=%fused_computation.21 | loop fusion | flops 2097152 | bytes 16777216 | tf_op jit(solution)/shard_map/stack | solution.py:110
  468.0 6.2 %bitcast_select_fusion = (f32[8192,256]{1,0:T(8,128)S(1)}, f32[8192,256]{1,0:T(8,128)}) fusion(f32[2,16,256,256]{3,2,1,0:T(8,128)} %pad_maximum_fusion.8, f32[2,32,128,256]{3,2,1,0:T(8,128)S(1)} %bitcast.366, pred[]{:T(512)S(6)} %eq.6), kind=kLoop, calls=%fused_computation.22 | loop fusion | flops 4194304 | bytes 33554432 | tf_op jit(solution)/shard_map/jit(_where)/select_n | solution.py:113
  475.6 7.8 %convolution_subtract_fusion = f32[8192,256]{1,0:T(8,128)} fusion(f32[8192,256]{1,0:T(8,128)} %get-tuple-element.35, f32[8192,256]{1,0:T(8,128)S(1)} %get-tuple-element.34, f32[256,256]{0,1:T(8,128)S(1)} %convolution_select_fusion), kind=kOutput, calls=%fused_computation.2 | convolution fusion | flops 3223322624 | bytes 25427968 | tf_op jit(solution)/shard_map/dot_general | solution.py:143
  483.4 10.2 %copy.134 = f32[2,32,128,256]{2,1,0,3:T(8,128)} copy(f32[2,32,128,256]{3,2,1,0:T(8,128)} %bitcast.373) | data formatting | bytes 16777216 | tf_op jit(solution)/shard_map/reshape | solution.py:144
  (375 shorter events, 205.5 us)
Async XLA Ops:
  11.6 19.4 %collective-permute-start.8 = (f32[2,1,128,256]{3,2,1,0:T(8,128)S(1)}, f32[2,1,128,256]{3,2,1,0:T(8,128)S(1)}, u32[]{:S(2)}, u32[]{:S(2)}) collective-permute-start(f32[2,1,128,256]{3,2,1,0:T(8,128)S(1)} %get-tuple-element.72), channel_id=1, source_target_pairs={{0,16},{16,0},{1,17},{17,1},{2,18},{18,2},{3,19},{19,3},{4,20},{20... | collective-permute-start | bytes 786440 | tf_op jit(solution)/shard_map/ppermute | solution.py:17
  53.9 9.2 %collective-permute-start.12 = (f32[2,1,128,256]{3,2,1,0:T(8,128)S(1)}, f32[2,1,128,256]{3,2,1,0:T(8,128)S(1)}, u32[]{:S(2)}, u32[]{:S(2)}) collective-permute-start(f32[2,1,128,256]{3,2,1,0:T(8,128)S(1)} %get-tuple-element.68), channel_id=1, source_target_pairs={{0,16},{16,0},{1,17},{17,1},{2,18},{18,2},{3,19},{19,3},{4,20},{20... | collective-permute-start | bytes 786440 | tf_op jit(solution)/shard_map/ppermute | solution.py:17
  54.0 9.2 %collective-permute-start.13 = (f32[2,1,128,256]{3,2,1,0:T(8,128)S(1)}, f32[2,1,128,256]{3,2,1,0:T(8,128)S(1)}, u32[]{:S(2)}, u32[]{:S(2)}) collective-permute-start(f32[2,1,128,256]{3,2,1,0:T(8,128)S(1)} %get-tuple-element.69), channel_id=1, source_target_pairs={{16,0},{0,16},{17,1},{1,17},{18,2},{2,18},{19,3},{3,19},{20,4},{4,... | collective-permute-start | bytes 786440 | tf_op jit(solution)/shard_map/ppermute | solution.py:22
  97.9 59.5 %collective-permute-start.52 = (f32[256,256]{0,1:T(8,128)S(1)}, f32[256,256]{0,1:T(8,128)}, u32[]{:S(2)}, u32[]{:S(2)}) collective-permute-start(f32[256,256]{0,1:T(8,128)S(1)} %convolution_bitcast_fusion), channel_id=1, source_target_pairs={{0,16},{16,0},{1,17},{17,1},{2,18},{18,2},{3,19},{19,3},{4,20},{20... | collective-permute-start | bytes 786440 | tf_op jit(solution)/shard_map/ppermute | solution.py:71
  98.7 61.3 %collective-permute-start.16 = (f32[256,256]{0,1:T(8,128)}, f32[256,256]{0,1:T(8,128)S(1)}, u32[]{:S(2)}, u32[]{:S(2)}) collective-permute-start(f32[256,256]{0,1:T(8,128)} %bitcast.414), channel_id=1, source_target_pairs={{0,1},{1,2},{2,3},{4,5},{5,6},{6,7},{8,9},{9,10},{10,11},{12,13},{... | collective-permute-start | bytes 786440 | tf_op jit(solution)/shard_map/ppermute | solution.py:102
  103.0 60.7 %collective-permute-start.34 = (f32[256,256]{0,1:T(8,128)}, f32[256,256]{0,1:T(8,128)S(1)}, u32[]{:S(2)}, u32[]{:S(2)}) collective-permute-start(f32[256,256]{0,1:T(8,128)} %bitcast.413), channel_id=1, source_target_pairs={{0,1},{1,2},{2,3},{4,5},{5,6},{6,7},{8,9},{9,10},{10,11},{12,13},{... | collective-permute-start | bytes 786440 | tf_op jit(solution)/shard_map/ppermute | solution.py:102
  158.3 10.2 %collective-permute-start.53 = (f32[256,256]{0,1:T(8,128)S(1)}, f32[256,256]{0,1:T(8,128)S(1)}, u32[]{:S(2)}, u32[]{:S(2)}) collective-permute-start(f32[256,256]{0,1:T(8,128)S(1)} %add.338), channel_id=1, source_target_pairs={{0,4},{4,0},{8,12},{12,8},{1,5},{5,1},{9,13},{13,9},{2,6},{6,2},{1... | collective-permute-start | bytes 786440 | tf_op jit(solution)/shard_map/ppermute | solution.py:71
  160.1 10.3 %collective-permute-start.17 = (f32[256,256]{0,1:T(8,128)S(1)}, f32[256,256]{0,1:T(8,128)S(1)}, u32[]{:S(2)}, u32[]{:S(2)}) collective-permute-start(f32[256,256]{0,1:T(8,128)S(1)} %bitcast_select_fusion.35), channel_id=1, source_target_pairs={{0,1},{1,2},{2,3},{4,5},{5,6},{6,7},{8,9},{9,10},{10,11},{12,13},{... | collective-permute-start | bytes 786440 | tf_op jit(solution)/shard_map/ppermute | solution.py:102
  163.8 12.3 %collective-permute-start.35 = (f32[256,256]{0,1:T(8,128)S(1)}, f32[256,256]{0,1:T(8,128)S(1)}, u32[]{:S(2)}, u32[]{:S(2)}) collective-permute-start(f32[256,256]{0,1:T(8,128)S(1)} %bitcast_select_fusion.18), channel_id=1, source_target_pairs={{0,1},{1,2},{2,3},{4,5},{5,6},{6,7},{8,9},{9,10},{10,11},{12,13},{... | collective-permute-start | bytes 786440 | tf_op jit(solution)/shard_map/ppermute | solution.py:102
  168.5 16.3 %collective-permute-start.54 = (f32[256,256]{0,1:T(8,128)S(1)}, f32[256,256]{0,1:T(8,128)S(1)}, u32[]{:S(2)}, u32[]{:S(2)}) collective-permute-start(f32[256,256]{0,1:T(8,128)S(1)} %add.339), channel_id=1, source_target_pairs={{0,8},{4,12},{8,0},{12,4},{1,9},{5,13},{9,1},{13,5},{2,10},{6,14},... | collective-permute-start | bytes 786440 | tf_op jit(solution)/shard_map/ppermute | solution.py:71
  170.5 16.3 %collective-permute-start.18 = (f32[256,256]{0,1:T(8,128)S(1)}, f32[256,256]{0,1:T(8,128)S(1)}, u32[]{:S(2)}, u32[]{:S(2)}) collective-permute-start(f32[256,256]{0,1:T(8,128)S(1)} %bitcast_select_fusion.34), channel_id=1, source_target_pairs={{0,1},{1,2},{2,3},{4,5},{5,6},{6,7},{8,9},{9,10},{10,11},{12,13},{... | collective-permute-start | bytes 786440 | tf_op jit(solution)/shard_map/ppermute | solution.py:102
  176.1 12.8 %collective-permute-start.36 = (f32[256,256]{0,1:T(8,128)S(1)}, f32[256,256]{0,1:T(8,128)S(1)}, u32[]{:S(2)}, u32[]{:S(2)}) collective-permute-start(f32[256,256]{0,1:T(8,128)S(1)} %bitcast_select_fusion.17), channel_id=1, source_target_pairs={{0,1},{1,2},{2,3},{4,5},{5,6},{6,7},{8,9},{9,10},{10,11},{12,13},{... | collective-permute-start | bytes 786440 | tf_op jit(solution)/shard_map/ppermute | solution.py:102
  184.8 11.8 %collective-permute-start.55 = (f32[256,256]{0,1:T(8,128)S(1)}, f32[256,256]{0,1:T(8,128)S(1)}, u32[]{:S(2)}, u32[]{:S(2)}) collective-permute-start(f32[256,256]{0,1:T(8,128)S(1)} %add.340), channel_id=1, source_target_pairs={{0,1},{1,2},{2,3},{4,5},{5,6},{6,7},{8,9},{9,10},{10,11},{12,13},{... | collective-permute-start | bytes 786440 | tf_op jit(solution)/shard_map/ppermute | solution.py:81
  186.8 12.3 %collective-permute-start.19 = (f32[256,256]{0,1:T(8,128)S(1)}, f32[256,256]{0,1:T(8,128)S(1)}, u32[]{:S(2)}, u32[]{:S(2)}) collective-permute-start(f32[256,256]{0,1:T(8,128)S(1)} %bitcast_select_fusion.33), channel_id=1, source_target_pairs={{0,1},{1,2},{2,3},{4,5},{5,6},{6,7},{8,9},{9,10},{10,11},{12,13},{... | collective-permute-start | bytes 786440 | tf_op jit(solution)/shard_map/ppermute | solution.py:102
  189.0 15.8 %collective-permute-start.37 = (f32[256,256]{0,1:T(8,128)S(1)}, f32[256,256]{0,1:T(8,128)S(1)}, u32[]{:S(2)}, u32[]{:S(2)}) collective-permute-start(f32[256,256]{0,1:T(8,128)S(1)} %bitcast_select_fusion.16), channel_id=1, source_target_pairs={{0,1},{1,2},{2,3},{4,5},{5,6},{6,7},{8,9},{9,10},{10,11},{12,13},{... | collective-permute-start | bytes 786440 | tf_op jit(solution)/shard_map/ppermute | solution.py:102
  196.7 18.1 %collective-permute-start.56 = (f32[256,256]{0,1:T(8,128)S(1)}, f32[256,256]{0,1:T(8,128)S(1)}, u32[]{:S(2)}, u32[]{:S(2)}) collective-permute-start(f32[256,256]{0,1:T(8,128)S(1)} %broadcast_select_fusion.1), channel_id=1, source_target_pairs={{0,1},{1,2},{2,3},{4,5},{5,6},{6,7},{8,9},{9,10},{10,11},{12,13},{... | collective-permute-start | bytes 786440 | tf_op jit(solution)/shard_map/ppermute | solution.py:81
  199.2 17.6 %collective-permute-start.20 = (f32[256,256]{0,1:T(8,128)S(1)}, f32[256,256]{0,1:T(8,128)S(1)}, u32[]{:S(2)}, u32[]{:S(2)}) collective-permute-start(f32[256,256]{0,1:T(8,128)S(1)} %bitcast_select_fusion.32), channel_id=1, source_target_pairs={{0,1},{1,2},{2,3},{4,5},{5,6},{6,7},{8,9},{9,10},{10,11},{12,13},{... | collective-permute-start | bytes 786440 | tf_op jit(solution)/shard_map/ppermute | solution.py:102
  204.8 16.8 %collective-permute-start.38 = (f32[256,256]{0,1:T(8,128)S(1)}, f32[256,256]{0,1:T(8,128)S(1)}, u32[]{:S(2)}, u32[]{:S(2)}) collective-permute-start(f32[256,256]{0,1:T(8,128)S(1)} %bitcast_select_fusion.15), channel_id=1, source_target_pairs={{0,1},{1,2},{2,3},{4,5},{5,6},{6,7},{8,9},{9,10},{10,11},{12,13},{... | collective-permute-start | bytes 786440 | tf_op jit(solution)/shard_map/ppermute | solution.py:102
  214.8 17.9 %collective-permute-start.57 = (f32[256,256]{0,1:T(8,128)S(1)}, f32[256,256]{0,1:T(8,128)S(1)}, u32[]{:S(2)}, u32[]{:S(2)}) collective-permute-start(f32[256,256]{0,1:T(8,128)S(1)} %broadcast_select_fusion), channel_id=1, source_target_pairs={{0,1},{1,2},{2,3},{4,5},{5,6},{6,7},{8,9},{9,10},{10,11},{12,13},{... | collective-permute-start | bytes 786440 | tf_op jit(solution)/shard_map/ppermute | solution.py:81
  217.5 77.6 %collective-permute-start.21 = (f32[256,256]{0,1:T(8,128)}, f32[256,256]{0,1:T(8,128)S(1)}, u32[]{:S(2)}, u32[]{:S(2)}) collective-permute-start(f32[256,256]{0,1:T(8,128)} %bitcast_select_fusion.31), channel_id=1, source_target_pairs={{0,1},{1,2},{2,3},{4,5},{5,6},{6,7},{8,9},{9,10},{10,11},{12,13},{... | collective-permute-start | bytes 786440 | tf_op jit(solution)/shard_map/ppermute | solution.py:102
  222.3 76.5 %collective-permute-start.39 = (f32[256,256]{0,1:T(8,128)}, f32[256,256]{0,1:T(8,128)S(1)}, u32[]{:S(2)}, u32[]{:S(2)}) collective-permute-start(f32[256,256]{0,1:T(8,128)} %bitcast_select_fusion.14), channel_id=1, source_target_pairs={{0,1},{1,2},{2,3},{4,5},{5,6},{6,7},{8,9},{9,10},{10,11},{12,13},{... | collective-permute-start | bytes 786440 | tf_op jit(solution)/shard_map/ppermute | solution.py:102
  296.9 13.0 %collective-permute-start.22 = (f32[256,256]{0,1:T(8,128)}, f32[256,256]{0,1:T(8,128)S(1)}, u32[]{:S(2)}, u32[]{:S(2)}) collective-permute-start(f32[256,256]{0,1:T(8,128)} %bitcast_select_fusion.30), channel_id=1, source_target_pairs={{0,1},{1,2},{2,3},{4,5},{5,6},{6,7},{8,9},{9,10},{10,11},{12,13},{... | collective-permute-start | bytes 786440 | tf_op jit(solution)/shard_map/ppermute | solution.py:102
  300.5 12.6 %collective-permute-start.40 = (f32[256,256]{0,1:T(8,128)}, f32[256,256]{0,1:T(8,128)S(1)}, u32[]{:S(2)}, u32[]{:S(2)}) collective-permute-start(f32[256,256]{0,1:T(8,128)} %bitcast_select_fusion.13), channel_id=1, source_target_pairs={{0,1},{1,2},{2,3},{4,5},{5,6},{6,7},{8,9},{9,10},{10,11},{12,13},{... | collective-permute-start | bytes 786440 | tf_op jit(solution)/shard_map/ppermute | solution.py:102
  311.1 9.4 %collective-permute-start.23 = (f32[256,256]{0,1:T(8,128)S(1)}, f32[256,256]{0,1:T(8,128)S(1)}, u32[]{:S(2)}, u32[]{:S(2)}) collective-permute-start(f32[256,256]{0,1:T(8,128)S(1)} %bitcast_select_fusion.29), channel_id=1, source_target_pairs={{0,1},{1,2},{2,3},{4,5},{5,6},{6,7},{8,9},{9,10},{10,11},{12,13},{... | collective-permute-start | bytes 786440 | tf_op jit(solution)/shard_map/ppermute | solution.py:102
  314.1 10.1 %collective-permute-start.41 = (f32[256,256]{0,1:T(8,128)S(1)}, f32[256,256]{0,1:T(8,128)S(1)}, u32[]{:S(2)}, u32[]{:S(2)}) collective-permute-start(f32[256,256]{0,1:T(8,128)S(1)} %bitcast_select_fusion.12), channel_id=1, source_target_pairs={{0,1},{1,2},{2,3},{4,5},{5,6},{6,7},{8,9},{9,10},{10,11},{12,13},{... | collective-permute-start | bytes 786440 | tf_op jit(solution)/shard_map/ppermute | solution.py:102
  321.5 10.0 %collective-permute-start.24 = (f32[256,256]{0,1:T(8,128)S(1)}, f32[256,256]{0,1:T(8,128)S(1)}, u32[]{:S(2)}, u32[]{:S(2)}) collective-permute-start(f32[256,256]{0,1:T(8,128)S(1)} %bitcast_select_fusion.28), channel_id=1, source_target_pairs={{0,1},{1,2},{2,3},{4,5},{5,6},{6,7},{8,9},{9,10},{10,11},{12,13},{... | collective-permute-start | bytes 786440 | tf_op jit(solution)/shard_map/ppermute | solution.py:102
  325.2 10.5 %collective-permute-start.42 = (f32[256,256]{0,1:T(8,128)S(1)}, f32[256,256]{0,1:T(8,128)S(1)}, u32[]{:S(2)}, u32[]{:S(2)}) collective-permute-start(f32[256,256]{0,1:T(8,128)S(1)} %bitcast_select_fusion.11), channel_id=1, source_target_pairs={{0,1},{1,2},{2,3},{4,5},{5,6},{6,7},{8,9},{9,10},{10,11},{12,13},{... | collective-permute-start | bytes 786440 | tf_op jit(solution)/shard_map/ppermute | solution.py:102
  332.5 9.9 %collective-permute-start.25 = (f32[256,256]{0,1:T(8,128)S(1)}, f32[256,256]{0,1:T(8,128)S(1)}, u32[]{:S(2)}, u32[]{:S(2)}) collective-permute-start(f32[256,256]{0,1:T(8,128)S(1)} %bitcast_select_fusion.27), channel_id=1, source_target_pairs={{0,1},{1,2},{2,3},{4,5},{5,6},{6,7},{8,9},{9,10},{10,11},{12,13},{... | collective-permute-start | bytes 786440 | tf_op jit(solution)/shard_map/ppermute | solution.py:102
  335.8 12.1 %collective-permute-start.43 = (f32[256,256]{0,1:T(8,128)S(1)}, f32[256,256]{0,1:T(8,128)S(1)}, u32[]{:S(2)}, u32[]{:S(2)}) collective-permute-start(f32[256,256]{0,1:T(8,128)S(1)} %bitcast_select_fusion.10), channel_id=1, source_target_pairs={{0,1},{1,2},{2,3},{4,5},{5,6},{6,7},{8,9},{9,10},{10,11},{12,13},{... | collective-permute-start | bytes 786440 | tf_op jit(solution)/shard_map/ppermute | solution.py:102
  342.5 12.1 %collective-permute-start.26 = (f32[256,256]{0,1:T(8,128)S(1)}, f32[256,256]{0,1:T(8,128)S(1)}, u32[]{:S(2)}, u32[]{:S(2)}) collective-permute-start(f32[256,256]{0,1:T(8,128)S(1)} %bitcast_select_fusion.26), channel_id=1, source_target_pairs={{0,1},{1,2},{2,3},{4,5},{5,6},{6,7},{8,9},{9,10},{10,11},{12,13},{... | collective-permute-start | bytes 786440 | tf_op jit(solution)/shard_map/ppermute | solution.py:102
  347.9 11.2 %collective-permute-start.44 = (f32[256,256]{0,1:T(8,128)S(1)}, f32[256,256]{0,1:T(8,128)S(1)}, u32[]{:S(2)}, u32[]{:S(2)}) collective-permute-start(f32[256,256]{0,1:T(8,128)S(1)} %bitcast_select_fusion.9), channel_id=1, source_target_pairs={{0,1},{1,2},{2,3},{4,5},{5,6},{6,7},{8,9},{9,10},{10,11},{12,13},{... | collective-permute-start | bytes 786440 | tf_op jit(solution)/shard_map/ppermute | solution.py:102
  354.6 11.2 %collective-permute-start.27 = (f32[256,256]{0,1:T(8,128)S(1)}, f32[256,256]{0,1:T(8,128)S(1)}, u32[]{:S(2)}, u32[]{:S(2)}) collective-permute-start(f32[256,256]{0,1:T(8,128)S(1)} %bitcast_select_fusion.25), channel_id=1, source_target_pairs={{0,1},{1,2},{2,3},{4,5},{5,6},{6,7},{8,9},{9,10},{10,11},{12,13},{... | collective-permute-start | bytes 786440 | tf_op jit(solution)/shard_map/ppermute | solution.py:102
  359.1 11.2 %collective-permute-start.45 = (f32[256,256]{0,1:T(8,128)S(1)}, f32[256,256]{0,1:T(8,128)S(1)}, u32[]{:S(2)}, u32[]{:S(2)}) collective-permute-start(f32[256,256]{0,1:T(8,128)S(1)} %bitcast_select_fusion.8), channel_id=1, source_target_pairs={{0,1},{1,2},{2,3},{4,5},{5,6},{6,7},{8,9},{9,10},{10,11},{12,13},{... | collective-permute-start | bytes 786440 | tf_op jit(solution)/shard_map/ppermute | solution.py:102
  365.8 11.2 %collective-permute-start.28 = (f32[256,256]{0,1:T(8,128)S(1)}, f32[256,256]{0,1:T(8,128)S(1)}, u32[]{:S(2)}, u32[]{:S(2)}) collective-permute-start(f32[256,256]{0,1:T(8,128)S(1)} %bitcast_select_fusion.24), channel_id=1, source_target_pairs={{0,1},{1,2},{2,3},{4,5},{5,6},{6,7},{8,9},{9,10},{10,11},{12,13},{... | collective-permute-start | bytes 786440 | tf_op jit(solution)/shard_map/ppermute | solution.py:102
  370.4 11.2 %collective-permute-start.46 = (f32[256,256]{0,1:T(8,128)S(1)}, f32[256,256]{0,1:T(8,128)S(1)}, u32[]{:S(2)}, u32[]{:S(2)}) collective-permute-start(f32[256,256]{0,1:T(8,128)S(1)} %bitcast_select_fusion.7), channel_id=1, source_target_pairs={{0,1},{1,2},{2,3},{4,5},{5,6},{6,7},{8,9},{9,10},{10,11},{12,13},{... | collective-permute-start | bytes 786440 | tf_op jit(solution)/shard_map/ppermute | solution.py:102
  377.1 11.4 %collective-permute-start.29 = (f32[256,256]{0,1:T(8,128)S(1)}, f32[256,256]{0,1:T(8,128)S(1)}, u32[]{:S(2)}, u32[]{:S(2)}) collective-permute-start(f32[256,256]{0,1:T(8,128)S(1)} %bitcast_select_fusion.23), channel_id=1, source_target_pairs={{0,1},{1,2},{2,3},{4,5},{5,6},{6,7},{8,9},{9,10},{10,11},{12,13},{... | collective-permute-start | bytes 786440 | tf_op jit(solution)/shard_map/ppermute | solution.py:102
  381.6 11.2 %collective-permute-start.47 = (f32[256,256]{0,1:T(8,128)S(1)}, f32[256,256]{0,1:T(8,128)S(1)}, u32[]{:S(2)}, u32[]{:S(2)}) collective-permute-start(f32[256,256]{0,1:T(8,128)S(1)} %bitcast_select_fusion.6), channel_id=1, source_target_pairs={{0,1},{1,2},{2,3},{4,5},{5,6},{6,7},{8,9},{9,10},{10,11},{12,13},{... | collective-permute-start | bytes 786440 | tf_op jit(solution)/shard_map/ppermute | solution.py:102
  388.5 11.0 %collective-permute-start.30 = (f32[256,256]{0,1:T(8,128)S(1)}, f32[256,256]{0,1:T(8,128)S(1)}, u32[]{:S(2)}, u32[]{:S(2)}) collective-permute-start(f32[256,256]{0,1:T(8,128)S(1)} %bitcast_select_fusion.22), channel_id=1, source_target_pairs={{0,1},{1,2},{2,3},{4,5},{5,6},{6,7},{8,9},{9,10},{10,11},{12,13},{... | collective-permute-start | bytes 786440 | tf_op jit(solution)/shard_map/ppermute | solution.py:102
  392.8 11.2 %collective-permute-start.48 = (f32[256,256]{0,1:T(8,128)S(1)}, f32[256,256]{0,1:T(8,128)S(1)}, u32[]{:S(2)}, u32[]{:S(2)}) collective-permute-start(f32[256,256]{0,1:T(8,128)S(1)} %bitcast_select_fusion.5), channel_id=1, source_target_pairs={{0,1},{1,2},{2,3},{4,5},{5,6},{6,7},{8,9},{9,10},{10,11},{12,13},{... | collective-permute-start | bytes 786440 | tf_op jit(solution)/shard_map/ppermute | solution.py:102
  399.5 11.2 %collective-permute-start.31 = (f32[256,256]{0,1:T(8,128)S(1)}, f32[256,256]{0,1:T(8,128)S(1)}, u32[]{:S(2)}, u32[]{:S(2)}) collective-permute-start(f32[256,256]{0,1:T(8,128)S(1)} %bitcast_select_fusion.21), channel_id=1, source_target_pairs={{0,1},{1,2},{2,3},{4,5},{5,6},{6,7},{8,9},{9,10},{10,11},{12,13},{... | collective-permute-start | bytes 786440 | tf_op jit(solution)/shard_map/ppermute | solution.py:102
  404.1 11.2 %collective-permute-start.49 = (f32[256,256]{0,1:T(8,128)S(1)}, f32[256,256]{0,1:T(8,128)S(1)}, u32[]{:S(2)}, u32[]{:S(2)}) collective-permute-start(f32[256,256]{0,1:T(8,128)S(1)} %bitcast_select_fusion.4), channel_id=1, source_target_pairs={{0,1},{1,2},{2,3},{4,5},{5,6},{6,7},{8,9},{9,10},{10,11},{12,13},{... | collective-permute-start | bytes 786440 | tf_op jit(solution)/shard_map/ppermute | solution.py:102
  410.8 11.1 %collective-permute-start.32 = (f32[256,256]{0,1:T(8,128)S(1)}, f32[256,256]{0,1:T(8,128)S(1)}, u32[]{:S(2)}, u32[]{:S(2)}) collective-permute-start(f32[256,256]{0,1:T(8,128)S(1)} %bitcast_select_fusion.20), channel_id=1, source_target_pairs={{0,1},{1,2},{2,3},{4,5},{5,6},{6,7},{8,9},{9,10},{10,11},{12,13},{... | collective-permute-start | bytes 786440 | tf_op jit(solution)/shard_map/ppermute | solution.py:102
  415.3 11.3 %collective-permute-start.50 = (f32[256,256]{0,1:T(8,128)S(1)}, f32[256,256]{0,1:T(8,128)S(1)}, u32[]{:S(2)}, u32[]{:S(2)}) collective-permute-start(f32[256,256]{0,1:T(8,128)S(1)} %bitcast_select_fusion.3), channel_id=1, source_target_pairs={{0,1},{1,2},{2,3},{4,5},{5,6},{6,7},{8,9},{9,10},{10,11},{12,13},{... | collective-permute-start | bytes 786440 | tf_op jit(solution)/shard_map/ppermute | solution.py:102
  422.0 11.3 %collective-permute-start.33 = (f32[256,256]{0,1:T(8,128)S(1)}, f32[256,256]{0,1:T(8,128)S(1)}, u32[]{:S(2)}, u32[]{:S(2)}) collective-permute-start(f32[256,256]{0,1:T(8,128)S(1)} %bitcast_select_fusion.19), channel_id=1, source_target_pairs={{0,1},{1,2},{2,3},{4,5},{5,6},{6,7},{8,9},{9,10},{10,11},{12,13},{... | collective-permute-start | bytes 786440 | tf_op jit(solution)/shard_map/ppermute | solution.py:102
  426.7 8.3 %collective-permute-start.51 = (f32[256,256]{0,1:T(8,128)S(1)}, f32[256,256]{0,1:T(8,128)S(1)}, u32[]{:S(2)}, u32[]{:S(2)}) collective-permute-start(f32[256,256]{0,1:T(8,128)S(1)} %bitcast_select_fusion.2), channel_id=1, source_target_pairs={{0,1},{1,2},{2,3},{4,5},{5,6},{6,7},{8,9},{9,10},{10,11},{12,13},{... | collective-permute-start | bytes 786440 | tf_op jit(solution)/shard_map/ppermute | solution.py:102
  436.3 21.4 %collective-permute-start.58 = (f32[256,256]{0,1:T(8,128)S(1)}, f32[256,256]{0,1:T(8,128)S(1)}, u32[]{:S(2)}, u32[]{:S(2)}) collective-permute-start(f32[256,256]{0,1:T(8,128)S(1)} %fusion.44), channel_id=1, source_target_pairs={{0,16},{16,0},{1,17},{17,1},{2,18},{18,2},{3,19},{19,3},{4,20},{20... | collective-permute-start | bytes 786440 | tf_op jit(solution)/shard_map/ppermute | solution.py:71
  457.7 8.8 %collective-permute-start.59 = (f32[256,256]{0,1:T(8,128)S(1)}, f32[256,256]{0,1:T(8,128)S(1)}, u32[]{:S(2)}, u32[]{:S(2)}) collective-permute-start(f32[256,256]{0,1:T(8,128)S(1)} %add.377), channel_id=1, source_target_pairs={{0,4},{4,0},{8,12},{12,8},{1,5},{5,1},{9,13},{13,9},{2,6},{6,2},{1... | collective-permute-start | bytes 786440 | tf_op jit(solution)/shard_map/ppermute | solution.py:71
  466.5 8.0 %collective-permute-start.60 = (f32[256,256]{0,1:T(8,128)S(1)}, f32[256,256]{0,1:T(8,128)S(1)}, u32[]{:S(2)}, u32[]{:S(2)}) collective-permute-start(f32[256,256]{0,1:T(8,128)S(1)} %add.378), channel_id=1, source_target_pairs={{0,8},{4,12},{8,0},{12,4},{1,9},{5,13},{9,1},{13,5},{2,10},{6,14},... | collective-permute-start | bytes 786440 | tf_op jit(solution)/shard_map/ppermute | solution.py:71
  (52 other events, 972.1 us)
